TPU v7x, 32 devices: a whole 2x2x4 slice. The times are simulated.
32 devices in a mesh: fsdp: 4 (over y, x), ctx: 8 (over z, core).
Axes of the slice: x: 2, y: 2, z: 4, core: 2. Of those that a mesh axis runs over, the one named last changes fastest.
Arguments:
- block_input: bfloat16 [8, 2048, 960], P('fsdp', 'ctx'), may hold values from -6 to 6
- query_weight: bfloat16 [960, 960], P('fsdp'), may hold values from -0.1875 to 0.1875
- key_matrix: bfloat16 [960, 320], P('fsdp'), may hold values from -0.1875 to 0.1875
- value_matrix: bfloat16 [960, 320], P('fsdp'), may hold values from -0.1875 to 0.1875
- out_weight: bfloat16 [960, 960], P('fsdp'), may hold values from -1.5 to 1.5
- gate_weight: bfloat16 [960, 2560], P('fsdp'), may hold values from -0.1875 to 0.1875
- up_weight: bfloat16 [960, 2560], P('fsdp'), may hold values from -0.1875 to 0.1875
- down_weight: bfloat16 [2560, 960], P('fsdp'), may hold values from -0.125 to 0.125
- attention_gain: bfloat16 [960], P('fsdp'), may hold values from 0.5 to 1.5
- feedforward_gain: bfloat16 [960], P('fsdp'), may hold values from 0.5 to 1.5
- cotangent: bfloat16 [8, 2048, 960], P('fsdp', 'ctx'), may hold values from -6 to 6
Outputs:
- block_output: bfloat16 [8, 2048, 960], P('fsdp', 'ctx')
- input_grad: bfloat16 [8, 2048, 960], P('fsdp', 'ctx')
- query_grad: float32 [960, 960], P('fsdp')
- key_grad: float32 [960, 320], P('fsdp')
- value_grad: float32 [960, 320], P('fsdp')
- out_grad: float32 [960, 960], P('fsdp')
- gate_grad: float32 [960, 2560], P('fsdp')
- up_grad: float32 [960, 2560], P('fsdp')
- down_grad: float32 [2560, 960], P('fsdp')
- attention_gain_grad: float32 [960], P('fsdp')
- feedforward_gain_grad: float32 [960], P('fsdp')
All inputs are finite; a program needn't handle non-finite values.
Results may differ from a plain program's by a relative error of at most 0.024.
Values may be sent and summed in bfloat16 or wider, within the bound.
No kernel may reach another device: no remote copies, remote signals or barrier semaphores. Data moves between devices by JAX's collectives and lax.ppermute only.
A program may use at most 192 MiB of HBM per device.

v0:
```python
import jax
import jax.numpy as jnp
from jax import lax
from jax.sharding import PartitionSpec as P

QUERY_HEAD_COUNT = 15
KEY_HEAD_COUNT = 5
HEAD_DIM = 64


eps_norm = 1e-05
rope_base = 100000.0
masked_score = -1e30


def shifted(value, axis, by):
    length = lax.axis_size(axis)
    pairs = [(i, i + by) for i in range(length) if 0 <= i + by < length]
    return lax.ppermute(value, axis, pairs)


def passed_along(value, axis, steps):
    count = lax.axis_size(axis)
    pairs = [(source, (source + steps) % count) for source in range(count)]
    return lax.ppermute(value, axis, pairs)


def rope_tables(positions, head_width):
    steps_half = jnp.arange(head_width // 2, dtype=jnp.float32)
    frequencies = rope_base ** (-2.0 * steps_half / head_width)
    angles = positions.astype(jnp.float32)[:, None] * frequencies[None, :]
    angles = jnp.concatenate([angles, angles], axis=-1)
    return (jnp.cos(angles), jnp.sin(angles))


def turn_half(field):
    middle_index = field.shape[-1] // 2
    return jnp.concatenate([-field[..., middle_index:], field[..., :middle_index]], axis=-1)


def apply_rotation(field, cosine_table, sine_table):
    return field * cosine_table[None, :, None, :] + turn_half(field) * sine_table[None, :, None, :]


def reverse_rotation(field, cosine_table, sine_table):
    return field * cosine_table[None, :, None, :] - turn_half(field * sine_table[None, :, None, :])


def norm_back(grad_normed, field, inverse, scale_gain):
    scaled = grad_normed * scale_gain
    gain_term = jnp.sum(grad_normed * field * inverse, axis=0)
    grad_field = inverse * scaled - field * inverse * inverse * inverse * jnp.mean(
        scaled * field, axis=-1, keepdims=True
    )
    return (grad_field, gain_term)


def split_into_heads(block, head_count, head_width):
    return block.reshape(block.shape[0], block.shape[1], head_count, head_width)


def block_scores(query_head_rows, key_block, query_pos, key_pos):
    key_head_rows = split_into_heads(key_block, query_head_rows.shape[2], query_head_rows.shape[4])
    raw_scores = (
        jnp.einsum(
            "srkge,stke->srkgt", query_head_rows, key_head_rows, preferred_element_type=jnp.float32
        )
        * 0.125
    )
    allowed = key_pos[None, :] <= query_pos[:, None]
    return (raw_scores, allowed[None, :, None, None, :])


def absorb(carry_state, query_head_rows, key_piece, query_pos, key_pos):
    running_max, run_total, summed = carry_state
    raw_scores, allowed = block_scores(query_head_rows, key_piece[0], query_pos, key_pos)
    raw_scores = jnp.where(allowed, raw_scores, masked_score)
    new_max = jnp.maximum(running_max, jnp.max(raw_scores, axis=-1))
    factor = jnp.exp(running_max - new_max)
    weights = jnp.where(allowed, jnp.exp(raw_scores - new_max[..., None]), 0.0)
    run_total = run_total * factor + jnp.sum(weights, axis=-1)
    value_head_rows = split_into_heads(
        key_piece[1], query_head_rows.shape[2], query_head_rows.shape[4]
    )
    summed = summed * factor[..., None] + jnp.einsum(
        "srkgt,stke->srkge",
        weights.astype(jnp.bfloat16),
        value_head_rows,
        preferred_element_type=jnp.float32,
    )
    return (new_max, run_total, summed)


def pull_back(grad_query, key_piece, saved, query_pos, key_pos):
    query_head_rows, attended_gradient, log_total, balance = saved
    raw_scores, allowed = block_scores(query_head_rows, key_piece[0], query_pos, key_pos)
    probabilities = jnp.where(allowed, jnp.exp(raw_scores - log_total[..., None]), 0.0)
    key_head_rows = split_into_heads(
        key_piece[0], query_head_rows.shape[2], query_head_rows.shape[4]
    )
    value_head_rows = split_into_heads(
        key_piece[1], query_head_rows.shape[2], query_head_rows.shape[4]
    )
    grad_probs = jnp.einsum(
        "srkge,stke->srkgt", attended_gradient, value_head_rows, preferred_element_type=jnp.float32
    )
    grad_scores = (probabilities * (grad_probs - balance[..., None])).astype(jnp.bfloat16)
    grad_query = (
        grad_query
        + jnp.einsum(
            "srkgt,stke->srkge", grad_scores, key_head_rows, preferred_element_type=jnp.float32
        )
        * 0.125
    )
    grad_keys = (
        jnp.einsum(
            "srkgt,srkge->stke", grad_scores, query_head_rows, preferred_element_type=jnp.float32
        )
        * 0.125
    )
    grad_values = jnp.einsum(
        "srkgt,srkge->stke",
        probabilities.astype(jnp.bfloat16),
        attended_gradient,
        preferred_element_type=jnp.float32,
    )
    shape_flat = (grad_keys.shape[0], grad_keys.shape[1], grad_keys.shape[2] * grad_keys.shape[3])
    return (grad_query, jnp.stack([grad_keys.reshape(shape_flat), grad_values.reshape(shape_flat)]))


def move_kv(key_value):
    return shifted(key_value, "ctx", 1)


def pass_grads(block_gradient):
    return passed_along(block_gradient.astype(jnp.bfloat16), "ctx", 1).astype(block_gradient.dtype)


def shards(
    block_input,
    query_weight,
    key_matrix,
    value_matrix,
    out_weight,
    gate_weight,
    up_weight,
    down_weight,
    attention_gain,
    feedforward_gain,
    cotangent,
):
    gathered = (
        lax.all_gather(query_weight, "fsdp", axis=0, tiled=True),
        lax.all_gather(key_matrix, "fsdp", axis=0, tiled=True),
        lax.all_gather(value_matrix, "fsdp", axis=0, tiled=True),
        lax.all_gather(out_weight, "fsdp", axis=0, tiled=True),
        lax.all_gather(gate_weight, "fsdp", axis=0, tiled=True),
        lax.all_gather(up_weight, "fsdp", axis=0, tiled=True),
        lax.all_gather(down_weight, "fsdp", axis=0, tiled=True),
        lax.all_gather(attention_gain, "fsdp", axis=0, tiled=True),
        lax.all_gather(feedforward_gain, "fsdp", axis=0, tiled=True),
    )
    (
        query_full,
        key_full,
        value_full,
        out_full,
        gate_full,
        up_full,
        down_full,
        gain_first,
        gain_second,
    ) = gathered
    gain_one = gain_first.astype(jnp.float32)
    gain_two = gain_second.astype(jnp.float32)
    sequence_count, total_row_count, model_width = block_input.shape
    token_rows = sequence_count * total_row_count
    query_group_width = QUERY_HEAD_COUNT // KEY_HEAD_COUNT
    ctx_rank = lax.axis_index("ctx")
    ctx_count = lax.axis_size("ctx")
    local_rows = jnp.arange(total_row_count, dtype=jnp.int32)
    positions = ctx_rank * total_row_count + local_rows
    cosine_table, sine_table = rope_tables(positions, HEAD_DIM)
    inputs = block_input.reshape(token_rows, model_width).astype(jnp.float32)
    inv_one = lax.rsqrt(jnp.mean(inputs * inputs, axis=-1, keepdims=True) + eps_norm)
    first_normed = (inputs * inv_one * gain_one).astype(jnp.bfloat16)
    query_lin = jnp.dot(first_normed, query_full, preferred_element_type=jnp.float32)
    key_linear = jnp.dot(first_normed, key_full, preferred_element_type=jnp.float32)
    value_head_rows = jnp.dot(first_normed, value_full, preferred_element_type=jnp.float32).astype(
        jnp.bfloat16
    )
    query_head_rows = apply_rotation(
        query_lin.reshape(sequence_count, total_row_count, QUERY_HEAD_COUNT, HEAD_DIM),
        cosine_table,
        sine_table,
    ).astype(jnp.bfloat16)
    query_head_rows = query_head_rows.reshape(
        sequence_count, total_row_count, KEY_HEAD_COUNT, query_group_width, HEAD_DIM
    )
    key_head_rows = apply_rotation(
        key_linear.reshape(sequence_count, total_row_count, KEY_HEAD_COUNT, HEAD_DIM),
        cosine_table,
        sine_table,
    ).astype(jnp.bfloat16)
    key_value = jnp.stack(
        [
            key_head_rows.reshape(sequence_count, total_row_count, KEY_HEAD_COUNT * HEAD_DIM),
            value_head_rows.reshape(sequence_count, total_row_count, KEY_HEAD_COUNT * HEAD_DIM),
        ]
    )
    statistic_shape = (sequence_count, total_row_count, KEY_HEAD_COUNT, query_group_width)
    initial = (
        jnp.full(statistic_shape, masked_score, jnp.float32),
        jnp.zeros(statistic_shape, jnp.float32),
        jnp.zeros(statistic_shape + (HEAD_DIM,), jnp.float32),
    )
    own_state = absorb(initial, query_head_rows, key_value, positions, positions)

    def fore_step(turn_index, carry):
        moving, carry_state = carry
        moving = move_kv(moving)
        source = (ctx_rank - turn_index) % ctx_count

        def fore_active(inner_state):
            return absorb(
                inner_state,
                query_head_rows,
                moving,
                positions,
                source * total_row_count + local_rows,
            )

        def fore_skipped(inner_state):
            return inner_state

        carry_state = lax.cond(source <= ctx_rank, fore_active, fore_skipped, carry_state)
        return (moving, carry_state)

    moved_last, final_state = lax.fori_loop(1, ctx_count, fore_step, (key_value, own_state))
    running_max, run_total, summed = final_state
    attended_full = summed / run_total[..., None]
    log_total = running_max + jnp.log(run_total)
    attended = attended_full.reshape(token_rows, QUERY_HEAD_COUNT * HEAD_DIM).astype(jnp.bfloat16)
    middle = inputs + jnp.dot(attended, out_full, preferred_element_type=jnp.float32)
    inv_two = lax.rsqrt(jnp.mean(middle * middle, axis=-1, keepdims=True) + eps_norm)
    normed_two = (middle * inv_two * gain_two).astype(jnp.bfloat16)
    gate_lin = jnp.dot(normed_two, gate_full, preferred_element_type=jnp.float32)
    up_lin = jnp.dot(normed_two, up_full, preferred_element_type=jnp.float32)
    sigmoid_gate = jax.nn.sigmoid(gate_lin)
    swish_gate = gate_lin * sigmoid_gate
    hidden = (swish_gate * up_lin).astype(jnp.bfloat16)
    final = middle + jnp.dot(hidden, down_full, preferred_element_type=jnp.float32)
    block_output = final.astype(jnp.bfloat16).reshape(sequence_count, total_row_count, model_width)
    grad_low = cotangent.reshape(token_rows, model_width)
    grad_out = grad_low.astype(jnp.float32)
    down_term = jnp.einsum("tf,td->fd", hidden, grad_low, preferred_element_type=jnp.float32)
    grad_hidden = jnp.einsum("td,fd->tf", grad_low, down_full, preferred_element_type=jnp.float32)
    grad_gate = (
        grad_hidden * up_lin * sigmoid_gate * (1.0 + gate_lin * (1.0 - sigmoid_gate))
    ).astype(jnp.bfloat16)
    grad_up = (grad_hidden * swish_gate).astype(jnp.bfloat16)
    gate_term = jnp.einsum("td,tf->df", normed_two, grad_gate, preferred_element_type=jnp.float32)
    up_term = jnp.einsum("td,tf->df", normed_two, grad_up, preferred_element_type=jnp.float32)
    grad_normed_two = jnp.einsum(
        "tf,df->td", grad_gate, gate_full, preferred_element_type=jnp.float32
    ) + jnp.einsum("tf,df->td", grad_up, up_full, preferred_element_type=jnp.float32)
    grad_field_two, gain_two_term = norm_back(grad_normed_two, middle, inv_two, gain_two)
    grad_middle = grad_out + grad_field_two
    grad_middle_low = grad_middle.astype(jnp.bfloat16)
    out_term = jnp.einsum(
        "tq,td->qd", attended, grad_middle_low, preferred_element_type=jnp.float32
    )
    attended_gradient = jnp.einsum(
        "td,qd->tq", grad_middle_low, out_full, preferred_element_type=jnp.float32
    ).astype(jnp.bfloat16)
    attended_gradient = attended_gradient.reshape(
        sequence_count, total_row_count, KEY_HEAD_COUNT, query_group_width, HEAD_DIM
    )
    balance = jnp.sum(attended_gradient.astype(jnp.float32) * attended_full, axis=-1)
    saved = (query_head_rows, attended_gradient, log_total, balance)
    query_zero = jnp.zeros(statistic_shape + (HEAD_DIM,), jnp.float32)
    grad_query, block_gradient = pull_back(query_zero, key_value, saved, positions, positions)

    def back_step(turn_index, carry):
        moving, grad_query_now, grad_block_now = carry
        moving = move_kv(moving)
        grad_block_now = pass_grads(grad_block_now)
        source = (ctx_rank - turn_index) % ctx_count

        def back_active(pair_grads):
            query_acc, block_acc = pair_grads
            query_acc, extra_grads = pull_back(
                query_acc, moving, saved, positions, source * total_row_count + local_rows
            )
            return (query_acc, block_acc + extra_grads)

        def back_skipped(pair_grads):
            return pair_grads

        grad_query_now, grad_block_now = lax.cond(
            source <= ctx_rank, back_active, back_skipped, (grad_query_now, grad_block_now)
        )
        return (moving, grad_query_now, grad_block_now)

    moved_back, grad_query, block_gradient = lax.fori_loop(
        1, ctx_count, back_step, (key_value, grad_query, block_gradient)
    )
    block_gradient = pass_grads(block_gradient)
    grad_key_lin = (
        reverse_rotation(
            split_into_heads(block_gradient[0], KEY_HEAD_COUNT, HEAD_DIM), cosine_table, sine_table
        )
        .astype(jnp.bfloat16)
        .reshape(token_rows, KEY_HEAD_COUNT * HEAD_DIM)
    )
    value_linear_gradient = (
        block_gradient[1].astype(jnp.bfloat16).reshape(token_rows, KEY_HEAD_COUNT * HEAD_DIM)
    )
    grad_query_lin = (
        reverse_rotation(
            grad_query.reshape(sequence_count, total_row_count, QUERY_HEAD_COUNT, HEAD_DIM),
            cosine_table,
            sine_table,
        )
        .astype(jnp.bfloat16)
        .reshape(token_rows, QUERY_HEAD_COUNT * HEAD_DIM)
    )
    query_term = jnp.einsum(
        "td,tq->dq", first_normed, grad_query_lin, preferred_element_type=jnp.float32
    )
    key_term = jnp.einsum(
        "td,tq->dq", first_normed, grad_key_lin, preferred_element_type=jnp.float32
    )
    value_term = jnp.einsum(
        "td,tq->dq", first_normed, value_linear_gradient, preferred_element_type=jnp.float32
    )
    grad_normed_one = jnp.einsum(
        "tq,dq->td", grad_query_lin, query_full, preferred_element_type=jnp.float32
    )
    grad_normed_one = grad_normed_one + jnp.einsum(
        "tq,dq->td", grad_key_lin, key_full, preferred_element_type=jnp.float32
    )
    grad_normed_one = grad_normed_one + jnp.einsum(
        "tq,dq->td", value_linear_gradient, value_full, preferred_element_type=jnp.float32
    )
    grad_field_one, gain_one_term = norm_back(grad_normed_one, inputs, inv_one, gain_one)
    input_grad = (
        (grad_middle + grad_field_one)
        .astype(jnp.bfloat16)
        .reshape(sequence_count, total_row_count, model_width)
    )
    shares = (
        lax.psum_scatter(
            query_term.astype(jnp.bfloat16), "fsdp", scatter_dimension=0, tiled=True
        ).astype(jnp.float32),
        lax.psum_scatter(
            key_term.astype(jnp.bfloat16), "fsdp", scatter_dimension=0, tiled=True
        ).astype(jnp.float32),
        lax.psum_scatter(
            value_term.astype(jnp.bfloat16), "fsdp", scatter_dimension=0, tiled=True
        ).astype(jnp.float32),
        lax.psum_scatter(
            out_term.astype(jnp.bfloat16), "fsdp", scatter_dimension=0, tiled=True
        ).astype(jnp.float32),
        lax.psum_scatter(
            gate_term.astype(jnp.bfloat16), "fsdp", scatter_dimension=0, tiled=True
        ).astype(jnp.float32),
        lax.psum_scatter(
            up_term.astype(jnp.bfloat16), "fsdp", scatter_dimension=0, tiled=True
        ).astype(jnp.float32),
        lax.psum_scatter(
            down_term.astype(jnp.bfloat16), "fsdp", scatter_dimension=0, tiled=True
        ).astype(jnp.float32),
        lax.psum_scatter(
            gain_one_term.astype(jnp.bfloat16), "fsdp", scatter_dimension=0, tiled=True
        ).astype(jnp.float32),
        lax.psum_scatter(
            gain_two_term.astype(jnp.bfloat16), "fsdp", scatter_dimension=0, tiled=True
        ).astype(jnp.float32),
    )
    totals = (
        lax.psum(shares[0].astype(jnp.bfloat16), "ctx").astype(jnp.float32),
        lax.psum(shares[1].astype(jnp.bfloat16), "ctx").astype(jnp.float32),
        lax.psum(shares[2].astype(jnp.bfloat16), "ctx").astype(jnp.float32),
        lax.psum(shares[3].astype(jnp.bfloat16), "ctx").astype(jnp.float32),
        lax.psum(shares[4].astype(jnp.bfloat16), "ctx").astype(jnp.float32),
        lax.psum(shares[5].astype(jnp.bfloat16), "ctx").astype(jnp.float32),
        lax.psum(shares[6].astype(jnp.bfloat16), "ctx").astype(jnp.float32),
        lax.psum(shares[7].astype(jnp.bfloat16), "ctx").astype(jnp.float32),
        lax.psum(shares[8].astype(jnp.bfloat16), "ctx").astype(jnp.float32),
    )
    return (
        block_output,
        input_grad,
        totals[0],
        totals[1],
        totals[2],
        totals[3],
        totals[4],
        totals[5],
        totals[6],
        totals[7],
        totals[8],
    )


def solution(mesh):
    in_specs = (
        P("fsdp", "ctx", None),
        P("fsdp", None),
        P("fsdp", None),
        P("fsdp", None),
        P("fsdp", None),
        P("fsdp", None),
        P("fsdp", None),
        P("fsdp", None),
        P("fsdp"),
        P("fsdp"),
        P("fsdp", "ctx", None),
    )
    out_specs = (
        P("fsdp", "ctx", None),
        P("fsdp", "ctx", None),
        P("fsdp", None),
        P("fsdp", None),
        P("fsdp", None),
        P("fsdp", None),
        P("fsdp", None),
        P("fsdp", None),
        P("fsdp", None),
        P("fsdp"),
        P("fsdp"),
    )
    return jax.shard_map(shards, mesh=mesh, in_specs=in_specs, out_specs=out_specs, check_vma=False)
```

profile of v0, /device:TPU:0, one launch (start us, length us, event | category | flops | bytes accessed | tf_op | source)
XLA Modules:
  0.0 1021.5 jit_solution(17117069851912748606)
XLA Ops:
  14.1 11.4 %all-reduce.9 = (bf16[960]{0:T(1024)(128)(2,1)S(1)}, bf16[960]{0:T(1024)(128)(2,1)S(1)}) all-reduce(bf16[960]{0:T(1024)(128)(2,1)S(1)} %dynamic-update-slice, bf16[960]{0:T(1024)(128)(2,1)S(1)} %dynamic-update-slice.1), channel_id=1, replica_groups=mesh['fsdp'=4,'ctx'=8] {'fsdp'}, use_global_device_ids=true, to_apply=%add | all-reduce | flops 1920 | bytes 7680
  27.5 13.8 %all-gather.1 = bf16[4,240,320]{1,2,0:T(8,128)(2,1)S(1)} all-gather(bf16[1,240,320]{1,2,0:T(8,128)(2,1)S(1)} %bitcast.339), channel_id=1, replica_groups=mesh['fsdp'=4,'ctx'=8] {'fsdp'}, dimensions={0}, use_global_device_ids=true | all-gather | bytes 768000 | tf_op jit(solution)/shard_map/all_gather | solution.py:155
  78.0 89.1 %while.42 = (s32[]{:T(128)}, bf16[2,2,256,320]{2,3,1,0:T(8,128)(2,1)S(1)}, f32[2,256,5,3]{1,3,2,0:T(4,128)S(1)}, f32[2,256,5,3]{1,3,2,0:T(4,128)S(1)}, f32[2,256...) while((s32[]{:T(128)}, ...), condition=%wide.region_8.9_spmd.clone, body=%wide.region_3.8_spmd.clone.sunk | while | flops 529939968 | bytes 50896368 | solution.py:239
  81.0 17.1 %collective-permute-start = (bf16[2,2,256,320]{2,3,1,0:T(8,128)(2,1)S(1)}, bf16[2,2,256,320]{2,3,1,0:T(8,128)(2,1)S(1)}, u32[]{:S(2)}, u32[]{:S(2)}) collective-permute-start(bf16[2,2,256,320]{2,3,1,0:T(8,128)(2,1)S(1)} %get-tuple-element.960), channel_id=1, source_target_pairs={{0,1},{1,2},{2,3},{3,4},{4,5},{5,6},{6,7},{8,9},{9,10},{10,11},{11... | collective-permute-start | bytes 1966088 | tf_op jit(solution)/shard_map/while/body/eval_jaxpr/ppermute | solution.py:19
  111.9 17.4 %collective-permute-start = (bf16[2,2,256,320]{2,3,1,0:T(8,128)(2,1)S(1)}, bf16[2,2,256,320]{2,3,1,0:T(8,128)(2,1)S(1)}, u32[]{:S(2)}, u32[]{:S(2)}) collective-permute-start(bf16[2,2,256,320]{2,3,1,0:T(8,128)(2,1)S(1)} %get-tuple-element.960), channel_id=1, source_target_pairs={{0,1},{1,2},{2,3},{3,4},{4,5},{5,6},{6,7},{8,9},{9,10},{10,11},{11... | collective-permute-start | bytes 1966088 | tf_op jit(solution)/shard_map/while/body/eval_jaxpr/ppermute | solution.py:19
  183.7 22.8 %all-gather.14.cloned.1.call-done = bf16[960,2560]{1,0:T(8,128)(2,1)} async-done(((bf16[240,2560]{1,0:T(8,128)(2,1)}), bf16[960,2560]{1,0:T(8,128)(2,1)}) %all-gather.14.cloned.1.call-update) | async-done | bytes 4915216 | tf_op jit(solution)/shard_map/all_gather | solution.py:158
  213.6 53.4 %all-gather.16.cloned.1.call-done = bf16[2560,960]{0,1:T(8,128)(2,1)} async-done(((bf16[640,960]{0,1:T(8,128)(2,1)}), bf16[2560,960]{0,1:T(8,128)(2,1)}) %all-gather.16.cloned.1.call-update) | async-done | bytes 4915216 | tf_op jit(solution)/shard_map/all_gather | solution.py:159
  307.8 223.0 %while.43 = (s32[]{:T(128)}, bf16[2,2,256,320]{2,3,1,0:T(8,128)(2,1)}, f32[2,256,5,3,64]{1,4,3,2,0:T(8,128)}, f32[2,2,256,320]{2,3,1,0:T(8,128)S(1)}, s32[]{:T(1...) while((s32[]{:T(128)}, ...), condition=%wide.region_15.16_spmd.clone, body=%wide.region_12.15_spmd.clone.sunk | while | flops 1280475648 | bytes 112690784 | solution.py:305
  324.1 21.0 %collective-permute-start.2 = (bf16[2,2,256,320]{2,3,1,0:T(8,128)(2,1)}, bf16[2,2,256,320]{2,3,1,0:T(8,128)(2,1)}, u32[]{:S(2)}, u32[]{:S(2)}) collective-permute-start(bf16[2,2,256,320]{2,3,1,0:T(8,128)(2,1)} %convert_element_type.398), channel_id=1, source_target_pairs={{0,1},{1,2},{2,3},{3,4},{4,5},{5,6},{6,7},{7,0},{8,9},{9,10},{10,1... | collective-permute-start | bytes 1966088 | tf_op jit(solution)/shard_map/while/body/eval_jaxpr/ppermute | solution.py:25
  353.0 11.1 %collective-permute-start.2 = (bf16[2,2,256,320]{2,3,1,0:T(8,128)(2,1)}, bf16[2,2,256,320]{2,3,1,0:T(8,128)(2,1)}, u32[]{:S(2)}, u32[]{:S(2)}) collective-permute-start(bf16[2,2,256,320]{2,3,1,0:T(8,128)(2,1)} %convert_element_type.398), channel_id=1, source_target_pairs={{0,1},{1,2},{2,3},{3,4},{4,5},{5,6},{6,7},{7,0},{8,9},{9,10},{10,1... | collective-permute-start | bytes 1966088 | tf_op jit(solution)/shard_map/while/body/eval_jaxpr/ppermute | solution.py:25
  364.1 22.2 %collective-permute-start.1 = (bf16[2,2,256,320]{2,3,1,0:T(8,128)(2,1)}, bf16[2,2,256,320]{2,3,1,0:T(8,128)(2,1)S(1)}, u32[]{:S(2)}, u32[]{:S(2)}) collective-permute-start(bf16[2,2,256,320]{2,3,1,0:T(8,128)(2,1)} %get-tuple-element.998), channel_id=1, source_target_pairs={{0,1},{1,2},{2,3},{3,4},{4,5},{5,6},{6,7},{8,9},{9,10},{10,11},{11... | collective-permute-start | bytes 1966088 | tf_op jit(solution)/shard_map/while/body/eval_jaxpr/ppermute | solution.py:19
  389.9 11.1 %collective-permute-start.2 = (bf16[2,2,256,320]{2,3,1,0:T(8,128)(2,1)}, bf16[2,2,256,320]{2,3,1,0:T(8,128)(2,1)}, u32[]{:S(2)}, u32[]{:S(2)}) collective-permute-start(bf16[2,2,256,320]{2,3,1,0:T(8,128)(2,1)} %convert_element_type.398), channel_id=1, source_target_pairs={{0,1},{1,2},{2,3},{3,4},{4,5},{5,6},{6,7},{7,0},{8,9},{9,10},{10,1... | collective-permute-start | bytes 1966088 | tf_op jit(solution)/shard_map/while/body/eval_jaxpr/ppermute | solution.py:25
  405.3 12.8 %collective-permute-done.2 = bf16[2,2,256,320]{2,3,1,0:T(8,128)(2,1)} collective-permute-done((bf16[2,2,256,320]{2,3,1,0:T(8,128)(2,1)}, bf16[2,2,256,320]{2,3,1,0:T(8,128)(2,1)}, u32[]{:S(2)}, u32[]{:S(2)}) %collective-permute-start.2) | collective-permute-done | bytes 655392 | tf_op jit(solution)/shard_map/while/body/eval_jaxpr/ppermute | solution.py:25
  436.3 18.7 %collective-permute-done.2 = bf16[2,2,256,320]{2,3,1,0:T(8,128)(2,1)} collective-permute-done((bf16[2,2,256,320]{2,3,1,0:T(8,128)(2,1)}, bf16[2,2,256,320]{2,3,1,0:T(8,128)(2,1)}, u32[]{:S(2)}, u32[]{:S(2)}) %collective-permute-start.2) | collective-permute-done | bytes 655392 | tf_op jit(solution)/shard_map/while/body/eval_jaxpr/ppermute | solution.py:25
  467.3 24.6 %collective-permute-done.2 = bf16[2,2,256,320]{2,3,1,0:T(8,128)(2,1)} collective-permute-done((bf16[2,2,256,320]{2,3,1,0:T(8,128)(2,1)}, bf16[2,2,256,320]{2,3,1,0:T(8,128)(2,1)}, u32[]{:S(2)}, u32[]{:S(2)}) %collective-permute-start.2) | collective-permute-done | bytes 655392 | tf_op jit(solution)/shard_map/while/body/eval_jaxpr/ppermute | solution.py:25
  496.2 32.5 %collective-permute-done.2 = bf16[2,2,256,320]{2,3,1,0:T(8,128)(2,1)} collective-permute-done((bf16[2,2,256,320]{2,3,1,0:T(8,128)(2,1)}, bf16[2,2,256,320]{2,3,1,0:T(8,128)(2,1)}, u32[]{:S(2)}, u32[]{:S(2)}) %collective-permute-start.2) | collective-permute-done | bytes 655392 | tf_op jit(solution)/shard_map/while/body/eval_jaxpr/ppermute | solution.py:25
  532.4 32.1 %collective-permute-done.3 = bf16[2,2,256,320]{2,3,1,0:T(8,128)(2,1)S(1)} collective-permute-done((bf16[2,2,256,320]{2,3,1,0:T(8,128)(2,1)S(1)}, bf16[2,2,256,320]{2,3,1,0:T(8,128)(2,1)S(1)}, u32[]{:S(2)}, u32[]{:S(2)}) %collective-permute-start.3) | collective-permute-done | bytes 655392 | tf_op jit(solution)/shard_map/ppermute | solution.py:25
  625.7 62.5 %reduce-scatter.18.cloned.1.call-done = bf16[640,960]{1,0:T(8,128)(2,1)} async-done(((bf16[2560,960]{1,0:T(8,128)(2,1)}), bf16[640,960]{1,0:T(8,128)(2,1)}) %reduce-scatter.18.cloned.1.call-update) | async-done | bytes 1228816
  690.6 34.8 %reduce-scatter.12.cloned.1.call-done = bf16[240,960]{1,0:T(8,128)(2,1)} async-done(((bf16[960,960]{1,0:T(8,128)(2,1)}), bf16[240,960]{1,0:T(8,128)(2,1)}) %reduce-scatter.12.cloned.1.call-update) | async-done | bytes 460816 | tf_op jit(solution)/shard_map/reduce_scatter | solution.py:362
  725.4 37.2 %reduce-scatter.10.cloned.1.call-done = bf16[240,960]{1,0:T(8,128)(2,1)} async-done(((bf16[960,960]{1,0:T(8,128)(2,1)}), bf16[240,960]{1,0:T(8,128)(2,1)}) %reduce-scatter.10.cloned.1.call-update) | async-done | bytes 460816 | tf_op jit(solution)/shard_map/reduce_scatter | solution.py:353
  762.6 61.6 %reduce-scatter.14.cloned.1.call-done = bf16[240,2560]{1,0:T(8,128)(2,1)} async-done(((bf16[960,2560]{1,0:T(8,128)(2,1)}), bf16[240,2560]{1,0:T(8,128)(2,1)}) %reduce-scatter.14.cloned.1.call-update) | async-done | bytes 1228816 | tf_op jit(solution)/shard_map/reduce_scatter | solution.py:365
  824.2 61.8 %reduce-scatter.16.cloned.1.call-done = bf16[240,2560]{1,0:T(8,128)(2,1)} async-done(((bf16[960,2560]{1,0:T(8,128)(2,1)}), bf16[240,2560]{1,0:T(8,128)(2,1)}) %reduce-scatter.16.cloned.1.call-update) | async-done | bytes 1228816 | tf_op jit(solution)/shard_map/reduce_scatter | solution.py:368
  910.1 15.6 %all-reduce.6 = (bf16[240]{0:T(256)(128)(2,1)S(1)}, bf16[240]{0:T(256)(128)(2,1)S(1)}) all-reduce(bf16[240]{0:T(256)(128)(2,1)S(1)} %dynamic-slice.7, bf16[240]{0:T(256)(128)(2,1)S(1)} %dynamic-slice.9), channel_id=1, replica_groups=mesh['fsdp'=4,'ctx'=8] {'ctx'}, use_global_device_ids=true, to_apply=%region_33.34 | all-reduce | flops 480 | bytes 1920 | tf_op jit(solution)/shard_map/psum | solution.py:389
  931.1 73.1 %all-reduce.14.cloned.1.call-done = (bf16[240,960]{1,0:T(8,128)(2,1)}, bf16[240,320]{0,1:T(8,128)(2,1)}, bf16[240,320]{0,1:T(8,128)(2,1)}, bf16[240,960]{1,0:T(8...) async-done(((bf16[240,960]{1,0:T(8,128)(2,1)}, bf16[240,320]{0,1:T(8,128)(2,1)}, bf16[240,320]{0,1:T(8,128)(2,1)}, ...) | async-done | bytes 4915216 | tf_op jit(solution)/shard_map/psum | solution.py:382
  (354 shorter events, 334.9 us)
Async XLA Ops:
  7.2 58.1 %all-gather.8.cloned.1.call-start = ((), (), s32[]{:S(2)}) async-start(), calls=%async_computation.5 | async-start | bytes 2457600 | tf_op jit(solution)/shard_map/all_gather | solution.py:153
  7.9 163.2 %all-gather.10.cloned.1.call-start = ((), (), s32[]{:S(2)}) async-start(), calls=%async_computation.6 | async-start | bytes 2457600 | tf_op jit(solution)/shard_map/all_gather | solution.py:156
  8.7 167.1 %all-gather.12.cloned.1.call-start = ((), (), s32[]{:S(2)}) async-start(), calls=%async_computation.7 | async-start | bytes 6144000 | tf_op jit(solution)/shard_map/all_gather | solution.py:157
  9.4 197.2 %all-gather.14.cloned.1.call-start = ((), (), s32[]{:S(2)}) async-start(), calls=%async_computation.8 | async-start | bytes 6144000 | tf_op jit(solution)/shard_map/all_gather | solution.py:158
  10.0 257.0 %all-gather.16.cloned.1.call-start = ((), (), s32[]{:S(2)}) async-start(), calls=%async_computation.9 | async-start | bytes 6144000 | tf_op jit(solution)/shard_map/all_gather | solution.py:159
  10.6 613.2 %all-reduce.16.cloned.1.call-start = ((), (), s32[]{:S(2)}) async-start(), calls=%async_computation.16 | async-start | bytes 2621440
  111.9 19.0 %collective-permute-start = (bf16[2,2,256,320]{2,3,1,0:T(8,128)(2,1)S(1)}, bf16[2,2,256,320]{2,3,1,0:T(8,128)(2,1)S(1)}, u32[]{:S(2)}, u32[]{:S(2)}) collective-permute-start(bf16[2,2,256,320]{2,3,1,0:T(8,128)(2,1)S(1)} %get-tuple-element.960), channel_id=1, source_target_pairs={{0,1},{1,2},{2,3},{3,4},{4,5},{5,6},{6,7},{8,9},{9,10},{10,11},{11... | collective-permute-start | bytes 1966088 | tf_op jit(solution)/shard_map/while/body/eval_jaxpr/ppermute | solution.py:19
  324.1 25.7 %collective-permute-start.2 = (bf16[2,2,256,320]{2,3,1,0:T(8,128)(2,1)}, bf16[2,2,256,320]{2,3,1,0:T(8,128)(2,1)}, u32[]{:S(2)}, u32[]{:S(2)}) collective-permute-start(bf16[2,2,256,320]{2,3,1,0:T(8,128)(2,1)} %convert_element_type.398), channel_id=1, source_target_pairs={{0,1},{1,2},{2,3},{3,4},{4,5},{5,6},{6,7},{7,0},{8,9},{9,10},{10,1... | collective-permute-start | bytes 1966088 | tf_op jit(solution)/shard_map/while/body/eval_jaxpr/ppermute | solution.py:25
  353.0 33.3 %collective-permute-start.2 = (bf16[2,2,256,320]{2,3,1,0:T(8,128)(2,1)}, bf16[2,2,256,320]{2,3,1,0:T(8,128)(2,1)}, u32[]{:S(2)}, u32[]{:S(2)}) collective-permute-start(bf16[2,2,256,320]{2,3,1,0:T(8,128)(2,1)} %convert_element_type.398), channel_id=1, source_target_pairs={{0,1},{1,2},{2,3},{3,4},{4,5},{5,6},{6,7},{7,0},{8,9},{9,10},{10,1... | collective-permute-start | bytes 1966088 | tf_op jit(solution)/shard_map/while/body/eval_jaxpr/ppermute | solution.py:25
  364.1 24.1 %collective-permute-start.1 = (bf16[2,2,256,320]{2,3,1,0:T(8,128)(2,1)}, bf16[2,2,256,320]{2,3,1,0:T(8,128)(2,1)S(1)}, u32[]{:S(2)}, u32[]{:S(2)}) collective-permute-start(bf16[2,2,256,320]{2,3,1,0:T(8,128)(2,1)} %get-tuple-element.998), channel_id=1, source_target_pairs={{0,1},{1,2},{2,3},{3,4},{4,5},{5,6},{6,7},{8,9},{9,10},{10,11},{11... | collective-permute-start | bytes 1966088 | tf_op jit(solution)/shard_map/while/body/eval_jaxpr/ppermute | solution.py:19
  389.9 28.2 %collective-permute-start.2 = (bf16[2,2,256,320]{2,3,1,0:T(8,128)(2,1)}, bf16[2,2,256,320]{2,3,1,0:T(8,128)(2,1)}, u32[]{:S(2)}, u32[]{:S(2)}) collective-permute-start(bf16[2,2,256,320]{2,3,1,0:T(8,128)(2,1)} %convert_element_type.398), channel_id=1, source_target_pairs={{0,1},{1,2},{2,3},{3,4},{4,5},{5,6},{6,7},{7,0},{8,9},{9,10},{10,1... | collective-permute-start | bytes 1966088 | tf_op jit(solution)/shard_map/while/body/eval_jaxpr/ppermute | solution.py:25
  421.1 33.9 %collective-permute-start.2 = (bf16[2,2,256,320]{2,3,1,0:T(8,128)(2,1)}, bf16[2,2,256,320]{2,3,1,0:T(8,128)(2,1)}, u32[]{:S(2)}, u32[]{:S(2)}) collective-permute-start(bf16[2,2,256,320]{2,3,1,0:T(8,128)(2,1)} %convert_element_type.398), channel_id=1, source_target_pairs={{0,1},{1,2},{2,3},{3,4},{4,5},{5,6},{6,7},{7,0},{8,9},{9,10},{10,1... | collective-permute-start | bytes 1966088 | tf_op jit(solution)/shard_map/while/body/eval_jaxpr/ppermute | solution.py:25
  431.9 24.2 %collective-permute-start.1 = (bf16[2,2,256,320]{2,3,1,0:T(8,128)(2,1)}, bf16[2,2,256,320]{2,3,1,0:T(8,128)(2,1)S(1)}, u32[]{:S(2)}, u32[]{:S(2)}) collective-permute-start(bf16[2,2,256,320]{2,3,1,0:T(8,128)(2,1)} %get-tuple-element.998), channel_id=1, source_target_pairs={{0,1},{1,2},{2,3},{3,4},{4,5},{5,6},{6,7},{8,9},{9,10},{10,11},{11... | collective-permute-start | bytes 1966088 | tf_op jit(solution)/shard_map/while/body/eval_jaxpr/ppermute | solution.py:19
  458.0 33.9 %collective-permute-start.2 = (bf16[2,2,256,320]{2,3,1,0:T(8,128)(2,1)}, bf16[2,2,256,320]{2,3,1,0:T(8,128)(2,1)}, u32[]{:S(2)}, u32[]{:S(2)}) collective-permute-start(bf16[2,2,256,320]{2,3,1,0:T(8,128)(2,1)} %convert_element_type.398), channel_id=1, source_target_pairs={{0,1},{1,2},{2,3},{3,4},{4,5},{5,6},{6,7},{7,0},{8,9},{9,10},{10,1... | collective-permute-start | bytes 1966088 | tf_op jit(solution)/shard_map/while/body/eval_jaxpr/ppermute | solution.py:25
  458.0 35.1 %collective-permute-start.1 = (bf16[2,2,256,320]{2,3,1,0:T(8,128)(2,1)}, bf16[2,2,256,320]{2,3,1,0:T(8,128)(2,1)S(1)}, u32[]{:S(2)}, u32[]{:S(2)}) collective-permute-start(bf16[2,2,256,320]{2,3,1,0:T(8,128)(2,1)} %get-tuple-element.998), channel_id=1, source_target_pairs={{0,1},{1,2},{2,3},{3,4},{4,5},{5,6},{6,7},{8,9},{9,10},{10,11},{11... | collective-permute-start | bytes 1966088 | tf_op jit(solution)/shard_map/while/body/eval_jaxpr/ppermute | solution.py:19
  494.9 33.9 %collective-permute-start.2 = (bf16[2,2,256,320]{2,3,1,0:T(8,128)(2,1)}, bf16[2,2,256,320]{2,3,1,0:T(8,128)(2,1)}, u32[]{:S(2)}, u32[]{:S(2)}) collective-permute-start(bf16[2,2,256,320]{2,3,1,0:T(8,128)(2,1)} %convert_element_type.398), channel_id=1, source_target_pairs={{0,1},{1,2},{2,3},{3,4},{4,5},{5,6},{6,7},{7,0},{8,9},{9,10},{10,1... | collective-permute-start | bytes 1966088 | tf_op jit(solution)/shard_map/while/body/eval_jaxpr/ppermute | solution.py:25
  494.9 35.1 %collective-permute-start.1 = (bf16[2,2,256,320]{2,3,1,0:T(8,128)(2,1)}, bf16[2,2,256,320]{2,3,1,0:T(8,128)(2,1)S(1)}, u32[]{:S(2)}, u32[]{:S(2)}) collective-permute-start(bf16[2,2,256,320]{2,3,1,0:T(8,128)(2,1)} %get-tuple-element.998), channel_id=1, source_target_pairs={{0,1},{1,2},{2,3},{3,4},{4,5},{5,6},{6,7},{8,9},{9,10},{10,11},{11... | collective-permute-start | bytes 1966088 | tf_op jit(solution)/shard_map/while/body/eval_jaxpr/ppermute | solution.py:19
  530.9 33.6 %collective-permute-start.3 = (bf16[2,2,256,320]{2,3,1,0:T(8,128)(2,1)S(1)}, bf16[2,2,256,320]{2,3,1,0:T(8,128)(2,1)S(1)}, u32[]{:S(2)}, u32[]{:S(2)}) collective-permute-start(bf16[2,2,256,320]{2,3,1,0:T(8,128)(2,1)S(1)} %convert_element_type.284), channel_id=1, source_target_pairs={{0,1},{1,2},{2,3},{3,4},{4,5},{5,6},{6,7},{7,0},{8,9},{9,10},{10,1... | collective-permute-start | bytes 1966088 | tf_op jit(solution)/shard_map/ppermute | solution.py:25
  569.6 118.5 %reduce-scatter.18.cloned.1.call-start = ((), (), s32[]{:S(2)}) async-start(), calls=%async_computation.14 | async-start | bytes 6553600
  583.7 141.6 %reduce-scatter.12.cloned.1.call-start = ((), (), s32[]{:S(2)}) async-start(), calls=%async_computation.11 | async-start | bytes 2457600 | tf_op jit(solution)/shard_map/reduce_scatter | solution.py:362
  589.0 173.6 %reduce-scatter.10.cloned.1.call-start = ((), (), s32[]{:S(2)}) async-start(), calls=%async_computation.10 | async-start | bytes 2457600 | tf_op jit(solution)/shard_map/reduce_scatter | solution.py:353
  596.4 227.8 %reduce-scatter.14.cloned.1.call-start = ((), (), s32[]{:S(2)}) async-start(), calls=%async_computation.12 | async-start | bytes 6144000 | tf_op jit(solution)/shard_map/reduce_scatter | solution.py:365
  603.6 282.4 %reduce-scatter.16.cloned.1.call-start = ((), (), s32[]{:S(2)}) async-start(), calls=%async_computation.13 | async-start | bytes 6144000 | tf_op jit(solution)/shard_map/reduce_scatter | solution.py:368
  610.6 393.6 %all-reduce.14.cloned.1.call-start = ((), (), s32[]{:S(2)}) async-start(), calls=%async_computation.15 | async-start | bytes 9994240 | tf_op jit(solution)/shard_map/psum | solution.py:382
  (67 other events, 606.8 us)
Sparse Core Ops, SparseCore 0:
  9.9 39.5 all-gather.7
  51.3 34.2 all-gather.9
  87.4 58.6 all-gather.11
  147.8 58.6 all-gather.13
  208.3 58.6 all-gather.15
  569.8 53.9 all-reduce.15
  626.7 61.4 reduce-scatter.17
  691.2 34.0 reduce-scatter.11
  728.4 34.0 reduce-scatter.9
  765.4 58.7 reduce-scatter.13
  827.2 58.7 reduce-scatter.15
  889.4 114.7 all-reduce.13
where the time goes:
time: 1030 us; the launch traced here: 1020 us
  waiting for transfers between devices  554 us (54%)
  starting transfers between devices  181 us (18%)
  matrix products  103 us (10%)
  local copies, waits for them, and re-layouts  62.8 us (6%)
  blocking collectives  60.3 us (6%)
  other arithmetic  42.7 us (4%)
  between operations  16.8 us (2%)
    ppermute x8, waiting for transfers between devices, passed_along(): return lax.ppermute(value, axis, pairs)  130 us
    ppermute x14, starting transfers between devices, shifted(): return lax.ppermute(value, axis, pairs)  126 us
    psum x1, waiting for transfers between devices, shards(): lax.psum(shares[0].astype(jnp.bfloat16), 'ctx').astype(jnp.float32)  73.1 us
    unnamed x14, waiting for transfers between devices  66.8 us
    reduce_scatter x1, waiting for transfers between devices, shards(): lax.psum_scatter(up_term.astype(jnp.bfloat16), 'fsdp', scatter_dimension=...  61.8 us
    reduce_scatter x1, waiting for transfers between devices, shards(): lax.psum_scatter(gate_term.astype(jnp.bfloat16), 'fsdp', scatter_dimensio...  61.6 us
    ppermute x8, starting transfers between devices, passed_along(): return lax.ppermute(value, axis, pairs)  54 us
    all_gather x1, waiting for transfers between devices, shards(): lax.all_gather(down_weight, 'fsdp', axis=0, tiled=True)  53.4 us
  transfers between devices with their start and end apart: 34, of which 25 were waited for; matrix products, arithmetic and copies ran while one was open for 13% of the time, Pallas kernels for 0%

commit v1 on v0

v1 whole, which is shorter than its diff:
```python
import functools

import jax
import jax.numpy as jnp
from jax import lax
from jax.experimental import pallas as pl
from jax.experimental.pallas import tpu as pltpu
from jax.sharding import PartitionSpec as P

QUERY_HEAD_COUNT = 15
KEY_HEAD_COUNT = 5
HEAD_DIM = 64
GROUP = QUERY_HEAD_COUNT // KEY_HEAD_COUNT

eps_norm = 1e-05
rope_base = 100000.0
masked_score = -1e30

f32 = jnp.float32
bf16 = jnp.bfloat16
AXES = ("fsdp", "ctx")
VMEM_BYTES = 48 * 1024 * 1024

NN = ((1,), (0,))
NT = ((1,), (1,))
TN = ((0,), (0,))


def dot(a, b, dims=NN):
    return lax.dot_general(a, b, (dims, ((), ())), preferred_element_type=f32)


def call(kernel, outs, args, flops, scratch=(), smem=0, hbm=(), outs_hbm=(), trans=0):
    specs = []
    for k in range(len(args)):
        if k < smem:
            specs.append(pl.BlockSpec(memory_space=pltpu.SMEM))
        elif k in hbm:
            specs.append(pl.BlockSpec(memory_space=pl.ANY))
        else:
            specs.append(pl.BlockSpec(memory_space=pltpu.VMEM))
    shapes = [jax.ShapeDtypeStruct(s, d) for s, d in outs]
    moved = sum(a.size * a.dtype.itemsize for a in args) + sum(
        s.size * s.dtype.itemsize for s in shapes
    )
    return pl.pallas_call(
        kernel,
        out_shape=shapes,
        in_specs=specs,
        out_specs=[
            pl.BlockSpec(memory_space=pl.ANY if k in outs_hbm else pltpu.VMEM)
            for k in range(len(shapes))
        ],
        scratch_shapes=list(scratch),
        compiler_params=pltpu.CompilerParams(vmem_limit_bytes=VMEM_BYTES),
        cost_estimate=pl.CostEstimate(
            flops=int(flops), bytes_accessed=int(moved), transcendentals=int(trans)
        ),
    )(*args)


def rotate_rows(part, cos, sin):
    half = HEAD_DIM // 2
    a, b = part[:half], part[half:]
    return jnp.concatenate([a * cos - b * sin, b * cos + a * sin], axis=0)


def unrotate_rows(part, cos, sin):
    half = HEAD_DIM // 2
    a, b = part[:half], part[half:]
    return jnp.concatenate([a * cos + b * sin, b * cos - a * sin], axis=0)


def run_copies(pairs, sems):
    copies = [pltpu.make_async_copy(a, b, sems.at[k]) for k, (a, b) in enumerate(pairs)]
    for copy in copies:
        copy.start()
    return copies


def placed(pieces, dst, order_ref, base, rows):
    pairs = []
    for s, piece in enumerate(pieces):
        if len(pieces) == 1:
            pairs.append((piece, dst))
        else:
            at = pl.multiple_of(order_ref[base + s] * rows, 16)
            pairs.append((piece.at[pl.ds(0, rows)], dst.at[pl.ds(at, rows)]))
    return pairs


def key_kernel(parts, slots, order_ref, x_ref, cos_ref, sin_ref, *refs):
    mine, theirs = refs[:parts], refs[parts : 2 * parts]
    refs = refs[2 * parts :]
    if parts == 1:
        gain_in, refs = refs[0], refs[1:]
    n1_ref, kv_ref, w_ref, gain_ref, gain_scr, sems = refs
    core = order_ref[0]
    width = x_ref.shape[1]
    rows = width // parts
    pairs = placed(mine, w_ref.at[core], order_ref, 1 + core * slots, rows)
    pairs += placed(theirs, w_ref.at[1 - core], order_ref, 1 + (1 - core) * slots, rows)
    if parts > 1:
        for s, piece in enumerate(mine):
            pairs.append((piece.at[pl.ds(rows, 16)], gain_scr.at[order_ref[1 + core * slots + s]]))
    copies = run_copies(pairs, sems)
    x = x_ref[...].astype(f32)
    inv = lax.rsqrt(jnp.mean(x * x, axis=-1, keepdims=True) + eps_norm)
    cos, sin = cos_ref[...], sin_ref[...]
    for copy in copies:
        copy.wait()
    if parts > 1:
        both = jnp.concatenate(
            [gain_scr[j].astype(f32)[:8, :rows] for j in range(parts)], axis=1
        )
    else:
        both = gain_in[...]
    gain_ref[...] = both
    n1_ref[...] = (x * inv * both[0:1, :]).astype(bf16)
    n1 = n1_ref[...]
    lin_t = dot(n1, w_ref[0]).T
    turned = [
        rotate_rows(lin_t[HEAD_DIM * h : HEAD_DIM * (h + 1)], cos, sin)
        for h in range(KEY_HEAD_COUNT)
    ]
    keys = jnp.concatenate(turned, axis=0).T.astype(bf16)
    values = dot(n1, w_ref[1]).astype(bf16)
    kv_ref[...] = jnp.concatenate([keys, values], axis=1)


def query_kernel(parts, slots, order_ref, n1_ref, cos_ref, sin_ref, *refs):
    mine, theirs = refs[:parts], refs[parts : 2 * parts]
    qt_ref, q_ref, wq_ref, wo_ref, sems = refs[2 * parts :]
    core = order_ref[0]
    rows = n1_ref.shape[1] // parts

    for c in range(2):

        @pl.when(core == c)
        def _():
            mine_to, theirs_to = (wq_ref, wo_ref) if c == 0 else (wo_ref, wq_ref)
            pairs = placed(mine, mine_to, order_ref, 1 + c * slots, rows)
            pairs += placed(theirs, theirs_to, order_ref, 1 + (1 - c) * slots, rows)
            for copy in run_copies(pairs, sems):
                copy.wait()

    cos, sin = cos_ref[...], sin_ref[...]
    lin_t = dot(n1_ref[...], wq_ref[...]).T
    for h in range(QUERY_HEAD_COUNT):
        turned = rotate_rows(lin_t[HEAD_DIM * h : HEAD_DIM * (h + 1)], cos, sin) * 0.125
        qt_ref[h] = turned.astype(bf16)
        q_ref[h] = turned.T.astype(bf16)


def halves_kernel(slots, order_ref, gate_ref, up_ref, down_ref, gu_ref, d_ref):
    ff = gate_ref.shape[1]
    step = ff // slots
    half = step // 2
    for c in range(2):

        @pl.when(order_ref[0] == c)
        def _():
            for j in range(slots):
                src = slice(step * j + half * c, step * j + half * (c + 1))
                gu_ref[:, half * j : half * (j + 1)] = gate_ref[:, src]
                gu_ref[:, ff // 2 + half * j : ff // 2 + half * (j + 1)] = up_ref[:, src]
            d_ref[...] = down_ref[half * c : half * (c + 1), :]


def forward_diagonal(qt_ref, kv_ref, m_ref, l_ref, acc_ref, k_scr, vt_scr):
    keys = kv_ref.shape[0]
    for g in range(KEY_HEAD_COUNT):
        k_scr[g] = kv_ref[:, HEAD_DIM * g : HEAD_DIM * (g + 1)]
        start = HEAD_DIM * (KEY_HEAD_COUNT + g)
        vt_scr[g] = kv_ref[:, start : start + HEAD_DIM].astype(f32).T.astype(bf16)
    m_ref[...] = jnp.zeros_like(m_ref)
    l_ref[...] = jnp.ones_like(l_ref)
    half = keys // 2

    @pl.loop(0, KEY_HEAD_COUNT)
    def _(g):
        for i in range(GROUP):
            h = g * GROUP + i
            for part in range(2):
                cols = slice(part * half, (part + 1) * half)
                used = (part + 1) * half
                st = dot(k_scr[g, :used, :], qt_ref[h, :, cols])
                key_at = lax.broadcasted_iota(jnp.int32, st.shape, 0)
                row_at = lax.broadcasted_iota(jnp.int32, st.shape, 1) + part * half
                st = jnp.where(key_at <= row_at, st, masked_score)
                top = jnp.max(st, axis=0, keepdims=True)
                p = jnp.exp(st - top)
                m_ref[g, i : i + 1, cols] = top
                l_ref[g, i : i + 1, cols] = jnp.sum(p, axis=0, keepdims=True)
                acc_ref[h, :, cols] = dot(vt_scr[g, :, :used], p.astype(bf16))


def forward_full(
    ok_ref, qt_ref, kv_ref, m_in, l_in, acc_in, m_ref, l_ref, acc_ref, k_scr, vt_scr
):
    m_ref[...] = m_in[...]
    l_ref[...] = l_in[...]

    @pl.when(ok_ref[0] == 0)
    def _():
        acc_ref[...] = acc_in[...]

    @pl.when(ok_ref[0] != 0)
    def _():
        for g in range(KEY_HEAD_COUNT):
            k_scr[g] = kv_ref[:, HEAD_DIM * g : HEAD_DIM * (g + 1)]
            start = HEAD_DIM * (KEY_HEAD_COUNT + g)
            vt_scr[g] = kv_ref[:, start : start + HEAD_DIM].astype(f32).T.astype(bf16)

        @pl.loop(0, KEY_HEAD_COUNT)
        def _(g):
            for i in range(GROUP):
                h = g * GROUP + i
                st = dot(k_scr[g], qt_ref[h])
                old = m_in[g, i : i + 1, :]
                top = jnp.maximum(old, jnp.max(st, axis=0, keepdims=True))
                factor = jnp.exp(old - top)
                p = jnp.exp(st - top)
                m_ref[g, i : i + 1, :] = top
                l_ref[g, i : i + 1, :] = l_in[g, i : i + 1, :] * factor + jnp.sum(
                    p, axis=0, keepdims=True
                )
                acc_ref[h] = acc_in[h] * factor + dot(vt_scr[g], p.astype(bf16))


def middle_kernel(x_ref, acc_ref, l_ref, wo_ref, gain_ref, att_ref, mid_ref, n2_ref):
    for h in range(QUERY_HEAD_COUNT):
        g, i = divmod(h, GROUP)
        att_ref[HEAD_DIM * h : HEAD_DIM * (h + 1), :] = (
            acc_ref[h] / l_ref[g, i : i + 1, :]
        ).astype(bf16)
    middle = x_ref[...].astype(f32) + dot(att_ref[...], wo_ref[...], TN)
    mid_ref[...] = middle
    inv = lax.rsqrt(jnp.mean(middle * middle, axis=-1, keepdims=True) + eps_norm)
    n2_ref[...] = (middle * inv * gain_ref[1:2, :]).astype(bf16)


def ff_kernel(parts, slots, groups, tile, order_ref, *refs):
    gu_pieces, d_pieces = refs[:parts], refs[parts : 2 * parts]
    n2m_ref, n2t_ref, cot_ref = refs[2 * parts : 2 * parts + 3]
    refs = refs[2 * parts + 3 :]
    out_ref, gn_ref, send_ref = refs[:3]
    gu_outs, d_outs = refs[3 : 3 + groups], refs[3 + groups : 3 + 2 * groups]
    wgu, wd, n2, turned, out, gn, ggu, gd, sems, out_sems = refs[3 + 2 * groups :]
    core = order_ref[0]
    width, ff2 = wgu.shape
    ff = ff2 // 2
    rows = n2m_ref.shape[0]
    base = 1 + core * slots
    copies = run_copies(
        placed(gu_pieces, wgu, order_ref, base, width // parts)
        + placed(d_pieces, wd, order_ref, base, ff // parts),
        sems,
    )
    n2[:rows, :] = n2m_ref[...]
    n2[rows:, :] = n2t_ref[...]
    turned[:, :rows] = n2m_ref[...].astype(f32).T.astype(bf16)
    turned[:, rows:] = n2t_ref[...].astype(f32).T.astype(bf16)
    out[...] = jnp.zeros_like(out)
    gn[...] = jnp.zeros_like(gn)
    for copy in copies:
        copy.wait()
    shard = width // slots

    @pl.loop(0, ff // tile)
    def _(step):
        at = pl.multiple_of(step * tile, tile)
        up_at = pl.multiple_of(ff + step * tile, 128)
        wg = wgu[:, pl.ds(at, tile)]
        wu = wgu[:, pl.ds(up_at, tile)]
        w_down = wd[pl.ds(at, tile), :]
        cot = cot_ref[...]
        gate = dot(n2[...], wg)
        up = dot(n2[...], wu)
        s = jax.nn.sigmoid(gate)
        swish = gate * s
        hidden = (swish * up).astype(bf16)
        grad_hidden = dot(cot, w_down, NT)
        grad_gate = (grad_hidden * up * s * (1.0 + gate * (1.0 - s))).astype(bf16)
        grad_up = (grad_hidden * swish).astype(bf16)
        out[...] += dot(hidden, w_down)
        gn[...] += dot(grad_gate, wg, NT) + dot(grad_up, wu, NT)
        gd[pl.ds(at, tile), :] = dot(hidden, cot, TN).astype(bf16)
        g_gate = dot(turned[...], grad_gate).astype(bf16)
        g_up = dot(turned[...], grad_up).astype(bf16)
        for j in range(slots):
            slot = order_ref[1 + (2 + core) * slots + j]
            ggu[slot, :, pl.ds(at, tile)] = g_gate[shard * j : shard * (j + 1)]
            ggu[slot, :, pl.ds(up_at, tile)] = g_up[shard * j : shard * (j + 1)]

    per = slots // groups
    down_rows = ff // slots
    pairs = [(ggu.at[pl.ds(per * k, per)], gu_outs[k]) for k in range(groups)]
    for s in range(slots):
        at = pl.multiple_of(order_ref[base + s] * down_rows, 16)
        pairs.append((gd.at[pl.ds(at, down_rows)], d_outs[s // per].at[s % per]))
    copies = run_copies(pairs, out_sems)
    out_ref[...] = out[:rows, :]
    gn_ref[...] = gn[:rows, :]
    send_ref[:, :width] = out[rows:, :].astype(bf16)
    send_ref[:, width:] = gn[rows:, :].astype(bf16)
    for copy in copies:
        copy.wait()


def turn_kernel(
    slots, order_ref, mid_ref, sum_ref, gn_ref, got_ref, gain_ref, cot_ref, wo_ref, att_ref,
    acc_ref, m_ref, l_ref,
    fin_ref, gm_ref, og_ref, og_send_ref, do_ref, dot_ref, del_ref, lse_ref, gg_ref,
):
    core = order_ref[0]
    middle = mid_ref[...]
    width = middle.shape[1]
    fin_ref[...] = (middle + sum_ref[...] + got_ref[:, :width].astype(f32)).astype(bf16)
    inv = lax.rsqrt(jnp.mean(middle * middle, axis=-1, keepdims=True) + eps_norm)
    gn = gn_ref[...] + got_ref[:, width:].astype(f32)
    gg_ref[...] = jnp.sum(gn * middle * inv, axis=0, keepdims=True)
    u = gn * gain_ref[1:2, :]
    gm = cot_ref[...].astype(f32) + inv * u - middle * (inv * inv * inv) * jnp.mean(
        u * middle, axis=-1, keepdims=True
    )
    gm_ref[...] = gm
    low = gm.astype(bf16)
    shard = width // slots
    split = og_ref.shape[2]
    og = dot(att_ref[...], low)
    for part in range(2):
        piece = og[:, :split] if part == 0 else og[:, split:]
        wide = piece.shape[1]
        for keep in range(2):
            ref = og_ref if keep else og_send_ref

            @pl.when((core == part) == (keep == 1))
            def _():
                if wide < split:
                    ref[:, :, wide:] = jnp.zeros((slots, shard, split - wide), bf16)
                for j in range(slots):
                    slot = order_ref[1 + (2 + part) * slots + j]
                    ref[slot, :, :wide] = piece[shard * j : shard * (j + 1)].astype(bf16)

    ga_t = dot(wo_ref[...], low, NT)
    del_ref[...] = jnp.zeros_like(del_ref)
    lse_ref[...] = m_ref[...] + jnp.log(l_ref[...])
    for h in range(QUERY_HEAD_COUNT):
        g, i = divmod(h, GROUP)
        part = ga_t[HEAD_DIM * h : HEAD_DIM * (h + 1)].astype(bf16)
        dot_ref[h] = part
        wide = part.astype(f32)
        do_ref[h] = wide.T.astype(bf16)
        del_ref[g, i : i + 1, :] = jnp.sum(
            wide * (acc_ref[h] / l_ref[g, i : i + 1, :]), axis=0, keepdims=True
        )


def backward_kernel(diagonal, first, *refs):
    if first:
        ok_ref, qt_ref, q_ref, dot_ref, do_ref, lse_ref, del_ref, kv_ref, dq_ref, dkv_ref, *scr = refs
        dq_in = None
    else:
        (
            ok_ref, qt_ref, q_ref, dot_ref, do_ref, lse_ref, del_ref, kv_ref, dq_in, dq_ref, dkv_ref, *scr,
        ) = refs
    k_scr, v_scr, kt_scr, dk_scr, dv_scr = scr
    keys = kv_ref.shape[0]

    @pl.when(ok_ref[0] == 0)
    def _():
        dq_ref[...] = jnp.zeros_like(dq_ref) if first else dq_in[...]
        dkv_ref[...] = jnp.zeros_like(dkv_ref)

    @pl.when(ok_ref[0] != 0)
    def _():
        for g in range(KEY_HEAD_COUNT):
            k = kv_ref[:, HEAD_DIM * g : HEAD_DIM * (g + 1)]
            k_scr[g] = k
            kt_scr[g] = k.astype(f32).T.astype(bf16)
            start = HEAD_DIM * (KEY_HEAD_COUNT + g)
            v_scr[g] = kv_ref[:, start : start + HEAD_DIM]

        parts = 2 if diagonal else 1
        rows = q_ref.shape[1]

        @pl.loop(0, KEY_HEAD_COUNT)
        def _(g):
            for part in range(parts):
                cols = slice(part * rows // parts, (part + 1) * rows // parts)
                used = (part + 1) * rows // parts if diagonal else keys
                dk = dv = None
                for i in range(GROUP):
                    h = g * GROUP + i
                    st = dot(k_scr[g, :used, :], qt_ref[h, :, cols])
                    p = jnp.exp(st - lse_ref[g, i : i + 1, cols])
                    if diagonal:
                        key_at = lax.broadcasted_iota(jnp.int32, st.shape, 0)
                        row_at = lax.broadcasted_iota(jnp.int32, st.shape, 1) + cols.start
                        p = jnp.where(key_at <= row_at, p, 0.0)
                    dpt = dot(v_scr[g, :used, :], dot_ref[h, :, cols])
                    ds = (p * (dpt - del_ref[g, i : i + 1, cols])).astype(bf16)
                    more_v = dot(p.astype(bf16), do_ref[h, cols, :])
                    more_k = dot(ds, q_ref[h, cols, :])
                    dv = more_v if dv is None else dv + more_v
                    dk = more_k if dk is None else dk + more_k
                    more_q = dot(kt_scr[g, :, :used], ds)
                    if first:
                        dq_ref[h, :, cols] = more_q
                    else:
                        dq_ref[h, :, cols] = dq_in[h, :, cols] + more_q
                if part == 0:
                    dk_scr[g, :used, :] = dk
                    dv_scr[g, :used, :] = dv
                else:
                    before = part * rows // parts
                    dk_scr[g, :before, :] += dk[:before]
                    dv_scr[g, :before, :] += dv[:before]
                    dk_scr[g, before:used, :] = dk[before:]
                    dv_scr[g, before:used, :] = dv[before:]

        dkv_ref[...] = jnp.concatenate(
            [dk_scr[g].astype(bf16) for g in range(KEY_HEAD_COUNT)]
            + [dv_scr[g].astype(bf16) for g in range(KEY_HEAD_COUNT)],
            axis=1,
        )


def last_kernel(
    slots, order_ref, dq_ref, dkv_ref, got_ref, n1_ref, wq_ref, w_ref, cos_ref, sin_ref, x_ref,
    gain_ref, gm_ref, gg_two_ref,
    ig_ref, keep_ref, send_ref, dqt_scr, n1t_scr, rhs_scr, gg_scr,
):
    core = order_ref[0]
    cos, sin = cos_ref[...], sin_ref[...]
    for h in range(QUERY_HEAD_COUNT):
        dqt_scr[HEAD_DIM * h : HEAD_DIM * (h + 1), :] = unrotate_rows(
            dq_ref[h] * 0.125, cos, sin
        ).astype(bf16)
    n1t_scr[...] = n1_ref[...].astype(f32).T.astype(bf16)
    n1t = n1t_scr[...]
    dqt = dqt_scr[...]
    width = dqt.shape[0]
    kv_width = KEY_HEAD_COUNT * HEAD_DIM
    cut = 2 * kv_width + width
    cut = keep_ref.shape[2]
    first = width - (cut - 2 * kv_width)
    dkv = dkv_ref[...].astype(f32) + got_ref[...].astype(f32)
    dk_t = dkv[:, :kv_width].T
    turned = [
        unrotate_rows(dk_t[HEAD_DIM * h : HEAD_DIM * (h + 1)], cos, sin)
        for h in range(KEY_HEAD_COUNT)
    ]
    dk = jnp.concatenate(turned, axis=0).T.astype(bf16)
    dv = dkv[:, kv_width:].astype(bf16)
    dq = dqt.astype(f32).T.astype(bf16)
    rhs_scr[:, : 2 * kv_width] = jnp.concatenate([dk, dv], axis=1)
    rhs_scr[:, 2 * kv_width :] = dq[:, first:]
    gn = dot(dq, wq_ref[...], NT) + dot(dk, w_ref[0], NT) + dot(dv, w_ref[1], NT)
    x = x_ref[...].astype(f32)
    inv = lax.rsqrt(jnp.mean(x * x, axis=-1, keepdims=True) + eps_norm)
    gg_one = jnp.sum(gn * x * inv, axis=0, keepdims=True)
    w = gn * gain_ref[0:1, :]
    ig_ref[...] = (
        gm_ref[...]
        + inv * w
        - x * (inv * inv * inv) * jnp.mean(w * x, axis=-1, keepdims=True)
    ).astype(bf16)
    shard = width // slots
    extra = keep_ref.shape[1] - shard
    row_at = lax.broadcasted_iota(jnp.int32, (extra, shard), 0)
    for j in range(slots):
        cols = slice(shard * j, shard * (j + 1))
        gg_scr[j, :, :] = jnp.zeros(gg_scr.shape[1:], f32)
        gg_scr[j, :, :shard] = jnp.where(
            row_at == 0, gg_one[:, cols], jnp.where(row_at == 1, gg_two_ref[:, cols], 0.0)
        )
    for part in range(2):
        if part == 0:
            piece = dot(n1t, dqt[:first], NT)
        else:
            piece = dot(n1t, rhs_scr[...])
        wide = piece.shape[1]
        for keep in range(2):
            ref = keep_ref if keep else send_ref

            @pl.when((core == part) == (keep == 1))
            def _():
                if wide < cut:
                    ref[:, :, wide:] = jnp.zeros((slots, shard + extra, cut - wide), bf16)
                for j in range(slots):
                    slot = order_ref[1 + (2 + part) * slots + j]
                    block = piece[shard * j : shard * (j + 1)]
                    tail = gg_scr[j] if part == 0 else jnp.zeros(gg_scr.shape[1:], f32)
                    ref[slot, :, :wide] = jnp.concatenate(
                        [block, tail[:, :wide]], axis=0
                    ).astype(bf16)


def finish_ff_kernel(
    slots, order_ref, gum_ref, gut_ref, dm_ref, dt_ref, om_ref, ot_ref,
    gate_ref, up_ref, down_ref, o_ref,
):
    ff = gate_ref.shape[1]
    step = ff // slots
    half = step // 2
    split = om_ref.shape[1]
    for core in range(2):

        @pl.when(order_ref[0] == core)
        def _():
            for c in range(2):
                gu, d, o = (gum_ref, dm_ref, om_ref) if c == core else (gut_ref, dt_ref, ot_ref)
                for j in range(slots):
                    dst = slice(step * j + half * c, step * j + half * (c + 1))
                    src = slice(half * j, half * (j + 1))
                    gate_ref[:, dst] = gu[:, src].astype(f32)
                    src = slice(ff // 2 + half * j, ff // 2 + half * (j + 1))
                    up_ref[:, dst] = gu[:, src].astype(f32)
                down_ref[half * c : half * (c + 1), :] = d[...].astype(f32)
                if c == 0:
                    o_ref[:, :split] = o[...].astype(f32)
                else:
                    o_ref[:, split:] = o[:, : o_ref.shape[1] - split].astype(f32)


def finish_kernel(chips, order_ref, *refs):
    mine, theirs = refs[:chips], refs[chips : 2 * chips]
    qg_ref, kg_ref, vg_ref, gg_ref, parts_scr = refs[2 * chips :]
    core = order_ref[0]
    place = order_ref[1]
    step = mine[0].shape[0]
    for k in range(chips):
        at = pl.multiple_of(lax.rem(place + chips - k, chips) * step, 16)
        parts_scr[core, pl.ds(at, step), :] = mine[k][...]
        parts_scr[1 - core, pl.ds(at, step), :] = theirs[k][...]
    shard, width = qg_ref.shape
    kv_width = kg_ref.shape[1]
    cut = parts_scr.shape[2]
    first = width - (cut - 2 * kv_width)
    qg_ref[:, :first] = parts_scr[0, :shard, :first].astype(f32)
    qg_ref[:, first:] = parts_scr[1, :shard, 2 * kv_width :].astype(f32)
    kg_ref[...] = parts_scr[1, :shard, :kv_width].astype(f32)
    vg_ref[...] = parts_scr[1, :shard, kv_width : 2 * kv_width].astype(f32)
    gg_ref[...] = parts_scr[0].astype(f32)[shard : shard + 8, :shard]


def moves(fsdp, ctx, target):
    pairs = []
    for f in range(fsdp):
        for c in range(ctx):
            to_f, to_c = target(f, c)
            if 0 <= to_c < ctx:
                pairs.append((f * ctx + c, to_f * ctx + to_c))
    return pairs


def plus(a, b):
    return (a.astype(f32) + b.astype(f32)).astype(bf16)


def program(
    fsdp, ctx,
    block_input, query_weight, key_matrix, value_matrix, out_weight, gate_weight, up_weight,
    down_weight, attention_gain, feedforward_gain, cotangent,
):
    chips = ctx // 2
    paired = fsdp == 4
    sibling = moves(fsdp, ctx, lambda f, c: (f, c ^ 1))
    up_z = moves(fsdp, ctx, lambda f, c: (f, c + 2))
    down_z = moves(fsdp, ctx, lambda f, c: (f, c - 2))
    near = moves(fsdp, ctx, lambda f, c: (f ^ (1 + c % 2), c))
    far = moves(fsdp, ctx, lambda f, c: (f ^ (2 - c % 2), c))
    rotations = [
        moves(fsdp, ctx, lambda f, c, k=k: (f, (c + 2 * k) % ctx)) for k in range(chips)
    ]
    columns = [[c + 2 * z for z in range(chips)] for c in range(2)]
    rank = lax.axis_index("ctx")
    core, place = rank % 2, rank // 2
    spot = lax.axis_index("fsdp")
    _, half, width = block_input.shape
    rows = 2 * half
    kv_width = KEY_HEAD_COUNT * HEAD_DIM
    shard = width // fsdp
    ff = gate_weight.shape[1]
    parts = fsdp if paired else 1

    def send(value, pairs):
        return lax.ppermute(value, AXES, pairs)

    ids = jnp.arange(fsdp, dtype=jnp.int32)
    if paired:
        first_order = jnp.bitwise_xor(spot, ids)
        swapped = jnp.array([0, 2, 1, 3], jnp.int32)
        second_order = jnp.bitwise_xor(spot, swapped)
        flip = jnp.bitwise_xor(spot, ids)
        second_slot = jnp.where(flip == 1, 2, jnp.where(flip == 2, 1, flip))
        order = [core[None], first_order, second_order, first_order, second_slot]
    else:
        order = [core[None], ids, ids, ids, ids]
    order = jnp.concatenate([o.astype(jnp.int32) for o in order])

    def gather(item):
        if not paired:
            return [lax.all_gather(item, "fsdp", axis=0, tiled=True)]
        a = send(item, near)
        b = send(item, far)
        return [item, a, b, send(a, far)]

    def swap_pieces(pieces, own):
        if not paired:
            return [send(pieces[0], sibling)]
        return [own] + [send(piece, sibling) for piece in pieces[1:]]

    def gather_pair(one, two):
        mine = gather(jnp.where(core == 0, one, two))
        return mine, swap_pieces(mine, jnp.where(core == 0, two, one))

    x_keep = lax.dynamic_index_in_dim(block_input, core, 0, keepdims=False)
    x_send = lax.dynamic_index_in_dim(block_input, 1 - core, 0, keepdims=False)
    x_got = send(x_send, sibling)
    x = jnp.concatenate(
        [jnp.where(core == 0, x_keep, x_got), jnp.where(core == 0, x_got, x_keep)], axis=0
    )

    def scatter_sequence(block):
        keep = lax.dynamic_slice_in_dim(block, core * half, half, 0)
        got = send(lax.dynamic_slice_in_dim(block, (1 - core) * half, half, 0), sibling)
        return jnp.stack([jnp.where(core == 0, keep, got), jnp.where(core == 0, got, keep)])

    positions = (place * rows + jnp.arange(rows, dtype=jnp.int32)).astype(f32)
    steps = jnp.arange(HEAD_DIM // 2, dtype=f32)
    angles = (rope_base ** (-2.0 * steps / HEAD_DIM))[:, None] * positions[None, :]
    cos, sin = jnp.cos(angles), jnp.sin(angles)

    if paired:
        gains = jnp.pad(
            jnp.stack([attention_gain, feedforward_gain]), ((0, 14), (0, kv_width - shard))
        )
        mine, theirs = gather_pair(
            jnp.concatenate([key_matrix, gains], axis=0),
            jnp.concatenate([value_matrix, gains], axis=0),
        )
        gain_args = ()
    else:
        mine, theirs = gather_pair(key_matrix, value_matrix)
        gains = jnp.stack([attention_gain, feedforward_gain])
        gains = lax.all_gather(gains.astype(f32), "fsdp", axis=1, tiled=True)
        gain_args = (jnp.pad(gains, ((0, 6), (0, 0))),)
    n1, kv, w_kv, gain = call(
        functools.partial(key_kernel, parts, fsdp),
        [
            ((rows, width), bf16),
            ((rows, 2 * kv_width), bf16),
            ((2, width, kv_width), bf16),
            ((8, width), f32),
        ],
        (order, x, cos, sin, *mine, *theirs, *gain_args),
        2 * rows * width * 2 * kv_width,
        scratch=[pltpu.VMEM((parts, 16, kv_width), bf16), pltpu.SemaphoreType.DMA((3 * parts,))],
        smem=1,
        hbm=range(4, 4 + 2 * parts),
    )

    blocks = [kv]
    for _ in range(1, chips):
        blocks.append(send(blocks[-1], up_z))

    mine, theirs = gather_pair(query_weight, out_weight)
    qt, q, wq, wo = call(
        functools.partial(query_kernel, parts, fsdp),
        [
            ((QUERY_HEAD_COUNT, HEAD_DIM, rows), bf16),
            ((QUERY_HEAD_COUNT, rows, HEAD_DIM), bf16),
            ((width, width), bf16),
            ((width, width), bf16),
        ],
        (order, n1, cos, sin, *mine, *theirs),
        2 * rows * width * width,
        scratch=[pltpu.SemaphoreType.DMA((2 * parts,))],
        smem=1,
        hbm=range(4, 4 + 2 * parts),
    )

    gate_up, down_half = call(
        functools.partial(halves_kernel, fsdp),
        [((shard, ff), bf16), ((down_weight.shape[0] // 2, width), bf16)],
        (order, gate_weight, up_weight, down_weight),
        0,
        smem=1,
    )
    gate_up = gather(gate_up)
    down_half = gather(down_half)

    stat = ((KEY_HEAD_COUNT, 8, rows), f32)
    acc_shape = ((QUERY_HEAD_COUNT, HEAD_DIM, rows), f32)
    key_scratch = pltpu.VMEM((KEY_HEAD_COUNT, rows, HEAD_DIM), bf16)
    turned_scratch = pltpu.VMEM((KEY_HEAD_COUNT, HEAD_DIM, rows), bf16)
    wide_scratch = pltpu.VMEM((KEY_HEAD_COUNT, rows, HEAD_DIM), f32)
    score_flops = 2 * rows * rows * width
    exps = rows * rows * QUERY_HEAD_COUNT

    def ok(distance):
        return (place >= distance).astype(jnp.int32)[None]

    m, l, acc = call(
        forward_diagonal,
        [stat, stat, acc_shape],
        (qt, kv),
        1.5 * score_flops,
        scratch=[key_scratch, turned_scratch],
        trans=exps,
    )
    for distance in range(1, chips):
        m, l, acc = call(
            forward_full,
            [stat, stat, acc_shape],
            (ok(distance), qt, blocks[distance], m, l, acc),
            2 * score_flops,
            scratch=[key_scratch, turned_scratch],
            smem=1,
            trans=exps,
        )

    att, middle, n2 = call(
        middle_kernel,
        [((width, rows), bf16), ((rows, width), f32), ((rows, width), bf16)],
        (x, acc, l, wo, gain),
        2 * rows * width * width,
    )

    n2_got = send(n2, sibling)
    cot_got = send(cotangent, sibling)
    cot_first = jnp.where(core == 0, cotangent, cot_got)
    cot_second = jnp.where(core == 0, cot_got, cotangent)
    cot_first = jnp.where(core == 0, cot_first, cot_first[::-1])
    cot_second = jnp.where(core == 0, cot_second, cot_second[::-1])
    cot = jnp.concatenate([cot_first, cot_second], axis=1).reshape(2 * rows, width)
    groups = 2 if paired else 1
    per = fsdp // groups
    half_ff = ff // 2
    down_rows = half_ff // fsdp
    tile = 256
    ff_out = call(
        functools.partial(ff_kernel, parts, fsdp, groups, tile),
        [((rows, width), f32), ((rows, width), f32), ((rows, 2 * width), bf16)]
        + [((per, shard, ff), bf16)] * groups
        + [((per, down_rows, width), bf16)] * groups,
        (order, *gate_up, *down_half, n2, n2_got, cot),
        18 * rows * width * ff,
        scratch=[
            pltpu.VMEM((width, ff), bf16),
            pltpu.VMEM((half_ff, width), bf16),
            pltpu.VMEM((2 * rows, width), bf16),
            pltpu.VMEM((width, 2 * rows), bf16),
            pltpu.VMEM((2 * rows, width), f32),
            pltpu.VMEM((2 * rows, width), f32),
            pltpu.VMEM((fsdp, shard, ff), bf16),
            pltpu.VMEM((half_ff, width), bf16),
            pltpu.SemaphoreType.DMA((2 * parts,)),
            pltpu.SemaphoreType.DMA((groups + fsdp,)),
        ],
        smem=1,
        hbm=range(1, 1 + 2 * parts),
        outs_hbm=range(3, 3 + 2 * groups),
        trans=2 * rows * half_ff,
    )
    ff_sum, gn, ff_send = ff_out[:3]
    gu_terms, down_terms = ff_out[3 : 3 + groups], ff_out[3 + groups :]
    ff_got = send(ff_send, sibling)

    split = 512
    final, grad_middle, o_keep, o_send, do, dot_t, delta, lse, gain_two_term = call(
        functools.partial(turn_kernel, fsdp),
        [
            ((rows, width), bf16),
            ((rows, width), f32),
            ((fsdp, shard, split), bf16),
            ((fsdp, shard, split), bf16),
            ((QUERY_HEAD_COUNT, rows, HEAD_DIM), bf16),
            ((QUERY_HEAD_COUNT, HEAD_DIM, rows), bf16),
            stat,
            stat,
            ((1, width), f32),
        ],
        (order, middle, ff_sum, gn, ff_got, gain, cot[:rows], wo, att, acc, m, l),
        4 * rows * width * width,
        smem=1,
    )

    def reduce_rows(terms):
        if not paired:
            return lax.psum_scatter(terms[0], "fsdp", scatter_dimension=0, tiled=False)
        total = plus(terms[0], send(terms[1], far))
        return plus(total[0], send(total[1], near))

    def grouped(term):
        return [term[per * k : per * (k + 1)] for k in range(groups)]

    gu_part = reduce_rows(gu_terms)
    down_part = reduce_rows(down_terms)
    o_part = reduce_rows(grouped(plus(o_keep, send(o_send, sibling))))
    gu_part, down_part, o_part = lax.psum(
        (gu_part, down_part, o_part), "ctx", axis_index_groups=columns
    )

    dq = None
    coming = None
    for distance in reversed(range(chips)):
        first = dq is None
        args = (ok(distance), qt, q, dot_t, do, lse, delta, blocks[distance])
        dq, dkv = call(
            functools.partial(backward_kernel, distance == 0, first),
            [acc_shape, ((rows, 2 * kv_width), bf16)],
            args if first else args + (dq,),
            5 * score_flops,
            scratch=[key_scratch, key_scratch, turned_scratch, wide_scratch, wide_scratch],
            smem=1,
            trans=exps,
        )
        if distance > 0:
            coming = send(dkv if coming is None else plus(dkv, coming), down_z)

    step = 16 * chips
    tail_rows = -(-(shard + 8) // step) * step
    cut = 832
    input_grad, keep, other = call(
        functools.partial(last_kernel, fsdp),
        [
            ((rows, width), bf16),
            ((fsdp, tail_rows, cut), bf16),
            ((fsdp, tail_rows, cut), bf16),
        ],
        (order, dq, dkv, coming, n1, wq, w_kv, cos, sin, x, gain, grad_middle, gain_two_term),
        4 * rows * width * (width + 2 * kv_width),
        scratch=[
            pltpu.VMEM((width, rows), bf16),
            pltpu.VMEM((width, rows), bf16),
            pltpu.VMEM((rows, cut), bf16),
            pltpu.VMEM((fsdp, tail_rows - shard, cut), f32),
        ],
        smem=1,
    )
    part = reduce_rows(grouped(plus(keep, send(other, sibling))))

    block = tail_rows // chips
    total = lax.dynamic_slice_in_dim(part, place * block, block, 0).astype(f32)
    for k in range(1, chips):
        to = (place + k) % chips
        piece = lax.dynamic_slice_in_dim(part, to * block, block, 0)
        total = total + send(piece, rotations[k]).astype(f32)
    total = total.astype(bf16)
    pieces = [total] + [send(total, rotations[k]) for k in range(1, chips)]
    other_pieces = [send(piece, sibling) for piece in pieces]
    query_grad, key_grad, value_grad, gain_grads = call(
        functools.partial(finish_kernel, chips),
        [
            ((shard, width), f32),
            ((shard, kv_width), f32),
            ((shard, kv_width), f32),
            ((8, shard), f32),
        ],
        (jnp.stack([core, place]).astype(jnp.int32), *pieces, *other_pieces),
        0,
        scratch=[pltpu.VMEM((2, tail_rows, cut), bf16)],
        smem=1,
    )
    gate_grad, up_grad, down_grad, out_grad = call(
        functools.partial(finish_ff_kernel, fsdp),
        [
            ((shard, ff), f32),
            ((shard, ff), f32),
            ((ff // fsdp, width), f32),
            ((shard, width), f32),
        ],
        (
            order, gu_part, send(gu_part, sibling), down_part, send(down_part, sibling),
            o_part, send(o_part, sibling),
        ),
        0,
        smem=1,
    )

    return (
        scatter_sequence(final),
        scatter_sequence(input_grad),
        query_grad,
        key_grad,
        value_grad,
        out_grad,
        gate_grad,
        up_grad,
        down_grad,
        gain_grads[0],
        gain_grads[1],
    )


def solution(mesh):
    in_specs = (
        P("fsdp", "ctx", None),
        P("fsdp", None),
        P("fsdp", None),
        P("fsdp", None),
        P("fsdp", None),
        P("fsdp", None),
        P("fsdp", None),
        P("fsdp", None),
        P("fsdp"),
        P("fsdp"),
        P("fsdp", "ctx", None),
    )
    out_specs = (
        P("fsdp", "ctx", None),
        P("fsdp", "ctx", None),
        P("fsdp", None),
        P("fsdp", None),
        P("fsdp", None),
        P("fsdp", None),
        P("fsdp", None),
        P("fsdp", None),
        P("fsdp", None),
        P("fsdp"),
        P("fsdp"),
    )
    body = functools.partial(program, mesh.shape["fsdp"], mesh.shape["ctx"])
    return jax.shard_map(body, mesh=mesh, in_specs=in_specs, out_specs=out_specs, check_vma=False)
```

time: 1030 us -> 500 us (0.49)
  waiting for transfers between devices: 554 us -> 215 us
  starting transfers between devices: 181 us -> 52.8 us
  Pallas kernels: 0 us -> 123 us
  matrix products: 103 us -> 0 us
  blocking collectives: 60.3 us -> 0 us
  other arithmetic: 42.7 us -> 29.9 us
    reduce_scatter x4 -> x0, waiting for transfers between devices: 195 us -> none  [the longest x1 61.8 us: shards(): lax.psum_scatter(up_term.astype(jnp.bfloat16), 'fsdp', scatter_dimension=...]
    ppermute x22 -> x53, starting transfers between devices: 180 us -> 52.8 us  [send(): return lax.ppermute(value, AXES, pairs)]
    pallas_call x0 -> x17, Pallas kernels: none -> 123 us  [call(): pl.pallas_call(kernel, out_shape=shapes, in_specs=specs, out_specs=[pl.Bl...]
    dot_general x27 -> x0, matrix products: 103 us -> none  [the longest x1 10.3 us: shards(): jnp.einsum('td,fd->tf', grad_low, down_full, preferred_element_type=jnp.f...]
    all_gather x5 -> x0, waiting for transfers between devices: 76.3 us -> none  [the longest x1 53.4 us: shards(): lax.all_gather(down_weight, 'fsdp', axis=0, tiled=True)]
    unnamed x14 -> x1, waiting for transfers between devices: 66.8 us -> 0.02 us
    all_gather x2 -> x0, blocking collectives: 24.3 us -> none  [the longest x1 13.8 us: shards(): lax.all_gather(value_matrix, 'fsdp', axis=0, tiled=True)]
    unnamed x2 -> x0, blocking collectives: 20.5 us -> none
  transfers between devices with their start and end apart: 34 -> 54, of which waited for: 25 -> 20; matrix products, arithmetic and copies ran while one was open for 13% -> 13% of each run, Pallas kernels for 0% -> 16%
where the time goes in v1:
time: 500 us; the launch traced here: 490 us
  waiting for transfers between devices  215 us (43%)
  Pallas kernels  123 us (25%)
  local copies, waits for them, and re-layouts  54.6 us (11%)
  starting transfers between devices  52.8 us (11%)
  other arithmetic  29.9 us (6%)
  between operations  15.3 us (3%)
    ppermute x53, waiting for transfers between devices, send(): return lax.ppermute(value, AXES, pairs)  141 us
    pallas_call x17, Pallas kernels, call(): pl.pallas_call(kernel, out_shape=shapes, in_specs=specs, out_specs=[pl.Bl...  123 us
    psum x1, waiting for transfers between devices, program(): lax.psum((gu_part, down_part, o_part), 'ctx', axis_index_groups=columns)  74.2 us
    ppermute x53, starting transfers between devices, send(): return lax.ppermute(value, AXES, pairs)  52.8 us
    unnamed x101, local copies, waits for them, and re-layouts  31.4 us
    convert_element_type x12, other arithmetic, plus(): return (a.astype(f32) + b.astype(f32)).astype(bf16)  16.9 us
  transfers between devices with their start and end apart: 54, of which 20 were waited for; matrix products, arithmetic and copies ran while one was open for 13% of the time, Pallas kernels for 16%

profile of v1, /device:TPU:0, one launch (start us, length us, event | category | flops | bytes accessed | tf_op | source)
XLA Modules:
  0.0 490.5 jit_solution(415087829673355392)
XLA Ops:
  21.5 3.8 collective-permute-done.3.refs_3_
  26.7 5.4 %shard_map.203 = (bf16[512,960]{1,0:T(8,128)(2,1)S(1)}, bf16[512,640]{1,0:T(8,128)(2,1)}, bf16[2,960,320]{2,1,0:T(8,128)(2,1)S(1)}, f32[8,960]{1,0:T(8,128)S(1)}) custom-call(s32[17]{0:T(128)S(1)} %concatenate.15.order_ref, bf16[512,960]{1,0:T(8,128)(2,1)S(1)} %pad_maximum_fusion.1.x_ref, f32[32,512]{1,0:T(8,128)S(1)} %get-tuple-element.176.cos_ref, ...), custom_call_target="tpu_custom_call" | custom-call | flops 629145600 | bytes 5322820 | tf_op jit(solution)/shard_map/pallas_call | solution.py:46
  33.3 4.3 collective-permute-start.13
  47.1 4.3 collective-permute-done.13.kv_ref.refs_7_
  51.4 5.2 %collective-permute-start.14 = (bf16[512,640]{1,0:T(8,128)(2,1)}, bf16[512,640]{1,0:T(8,128)(2,1)}, u32[]{:S(2)}, u32[]{:S(2)}) collective-permute-start(bf16[512,640]{1,0:T(8,128)(2,1)} %collective-permute-done.13.kv_ref.refs_7_), channel_id=1, source_target_pairs={{0,2},{1,3},{2,4},{3,5},{4,6},{5,7},{8,10},{9,11},{10,12},{11,13},... | collective-permute-start | bytes 1966088 | tf_op jit(solution)/shard_map/ppermute | solution.py:590
  60.8 10.1 %collective-permute-done.9.refs_3_ = bf16[240,960]{1,0:T(8,128)(2,1)S(1)} collective-permute-done((bf16[240,960]{1,0:T(8,128)(2,1)}, bf16[240,960]{1,0:T(8,128)(2,1)S(1)}, u32[]{:S(2)}, u32[]{:S(2)}) %collective-permute-start.9) | collective-permute-done | bytes 460832 | tf_op jit(solution)/shard_map/ppermute | solution.py:590
  70.9 3.8 collective-permute-start.15
  81.4 7.4 %shard_map.204 = (bf16[15,64,512]{2,1,0:T(8,128)(2,1)S(1)}, bf16[15,512,64]{2,1,0:T(8,128)(2,1)}, bf16[960,960]{1,0:T(8,128)(2,1)}, bf16[960,960]{1,0:T(8,128)(2,1)}) custom-call(s32[17]{0:T(128)S(1)} %concatenate.15.order_ref, bf16[512,960]{1,0:T(8,128)(2,1)S(1)} %copy-done.5, f32[32,512]{1,0:T(8,128)S(1)} %get-tuple-element.176.cos_ref, ...), custom_call_target="tpu_custom_call" | custom-call | flops 943718400 | bytes 10453060 | tf_op jit(solution)/shard_map/pallas_call | solution.py:46
  88.8 10.8 %shard_map.205 = (f32[5,8,512]{2,1,0:T(8,128)S(1)}, f32[5,8,512]{2,1,0:T(8,128)S(1)}, f32[15,64,512]{2,1,0:T(8,128)S(1)}) custom-call(bf16[15,64,512]{2,1,0:T(8,128)(2,1)S(1)} %get-tuple-element.72.qt_ref.refs_1_, bf16[512,640]{1,0:T(8,128)(2,1)} %get-tuple-element.73.kv_ref.refs_7_), custom_call_target="tpu_custom_call" | custom-call | flops 754974720 | bytes 3768320 | tf_op jit(solution)/shard_map/pallas_call | solution.py:46
  103.7 5.0 %shard_map.209 = (bf16[960,512]{1,0:T(8,128)(2,1)S(1)}, f32[512,960]{1,0:T(8,128)}, bf16[512,960]{1,0:T(8,128)(2,1)S(1)}) custom-call(bf16[512,960]{1,0:T(8,128)(2,1)S(1)} %pad_maximum_fusion.1.x_ref, f32[15,64,512]{2,1,0:T(8,128)S(1)} %get-tuple-element.83.acc_ref, f32[5,8,512]{2,1,0:T(8,128)S(1)} %get-tuple-element.84.l_ref, ...), custom_call_target="tpu_custom_call" | custom-call | flops 943718400 | bytes 8837120 | tf_op jit(solution)/shard_map/pallas_call | solution.py:46
  123.3 7.0 %collective-permute-done.21.refs_7_ = bf16[320,960]{1,0:T(8,128)(2,1)} collective-permute-done((bf16[320,960]{1,0:T(8,128)(2,1)}, bf16[320,960]{1,0:T(8,128)(2,1)}, u32[]{:S(2)}, u32[]{:S(2)}) %collective-permute-start.21) | collective-permute-done | bytes 614432 | tf_op jit(solution)/shard_map/ppermute | solution.py:590
  130.4 36.5 %shard_map.211 = (f32[512,960]{1,0:T(8,128)}, f32[512,960]{1,0:T(8,128)}, bf16[512,1920]{1,0:T(8,128)(2,1)}, bf16[2,240,2560]{2,1,0:T(8,128)(2,1)}, bf16[2,240,2...) custom-call(s32[17]{0:T(128)S(1)} %concatenate.15.order_ref, ...), custom_call_target="tpu_custom_call" | custom-call | flops 22649241600 | bytes 24576068 | tf_op jit(solution)/shard_map/pallas_call | solution.py:46
  171.4 13.4 %collective-permute-done.46 = bf16[2,320,960]{2,1,0:T(8,128)(2,1)S(1)} collective-permute-done((bf16[2,320,960]{2,1,0:T(8,128)(2,1)}, bf16[2,320,960]{2,1,0:T(8,128)(2,1)S(1)}, u32[]{:S(2)}, u32[]{:S(2)}) %collective-permute-start.46) | collective-permute-done | bytes 1228832 | tf_op jit(solution)/shard_map/ppermute | solution.py:590
  189.5 10.9 %shard_map.212 = (bf16[512,960]{1,0:T(8,128)(2,1)S(1)}, f32[512,960]{1,0:T(8,128)}, bf16[4,240,512]{2,1,0:T(8,128)(2,1)S(1)}, bf16[4,240,512]{2,1,0:T(8,128)(2,1...) custom-call(s32[17]{0:T(128)S(1)} %concatenate.15.order_ref, ...), custom_call_target="tpu_custom_call" | custom-call | flops 1887436800 | bytes 20883268 | tf_op jit(solution)/shard_map/pallas_call | solution.py:46
  214.3 13.7 %shard_map.216 = (f32[15,64,512]{2,1,0:T(8,128)S(1)}, bf16[512,640]{1,0:T(8,128)(2,1)S(1)}) custom-call(s32[1]{0:T(128)} %bitcast.10.refs_0_, bf16[15,64,512]{2,1,0:T(8,128)(2,1)S(1)} %copy-done.21, bf16[15,512,64]{2,1,0:T(8,128)(2,1)} %get-tuple-element.97.refs_2_, bf16[15,64,512]{2,1,0:T(8,128)(2,1)S(1)} %get-tuple-element.98.refs_3_, ...), custom_call_target="tpu_custom_call" | custom-call | flops 2516582400 | bytes 9338884 | tf_op jit(solution)/shard_map/pallas_call | solution.py:46
  236.8 29.4 %collective-permute-done.27 = bf16[512,640]{1,0:T(8,128)(2,1)S(1)} collective-permute-done((bf16[512,640]{1,0:T(8,128)(2,1)S(1)}, bf16[512,640]{1,0:T(8,128)(2,1)S(1)}, u32[]{:S(2)}, u32[]{:S(2)}) %collective-permute-start.27) | collective-permute-done | bytes 655392 | tf_op jit(solution)/shard_map/ppermute | solution.py:590
  270.3 33.8 %collective-permute-done.28.got_ref = bf16[512,640]{1,0:T(8,128)(2,1)S(1)} collective-permute-done((bf16[512,640]{1,0:T(8,128)(2,1)S(1)}, bf16[512,640]{1,0:T(8,128)(2,1)S(1)}, u32[]{:S(2)}, u32[]{:S(2)}) %collective-permute-start.28) | collective-permute-done | bytes 655392 | tf_op jit(solution)/shard_map/ppermute | solution.py:590
  304.1 10.8 %shard_map.217 = (bf16[512,960]{1,0:T(8,128)(2,1)S(1)}, bf16[4,256,832]{2,1,0:T(8,128)(2,1)}, bf16[4,256,832]{2,1,0:T(8,128)(2,1)}) custom-call(s32[17]{0:T(128)S(1)} %concatenate.15.order_ref, f32[15,64,512]{2,1,0:T(8,128)} %copy-done.22, bf16[512,640]{1,0:T(8,128)(2,1)S(1)} %get-tuple-element.106.dkv_ref, ...), custom_call_target="tpu_custom_call" | custom-call | flops 3145728000 | bytes 14837572 | tf_op jit(solution)/shard_map/pallas_call | solution.py:46
  314.9 3.6 copy.47
  339.2 12.0 %collective-permute-done.31 = bf16[2,256,832]{1,2,0:T(8,128)(2,1)} collective-permute-done((bf16[2,256,832]{1,2,0:T(8,128)(2,1)}, bf16[2,256,832]{1,2,0:T(8,128)(2,1)}, u32[]{:S(2)}, u32[]{:S(2)}) %collective-permute-start.31) | collective-permute-done | bytes 852000 | tf_op jit(solution)/shard_map/ppermute | solution.py:590
  359.9 74.2 %all-reduce.4.cloned.1.call-done = (bf16[240,2560]{1,0:T(8,128)(2,1)}, bf16[320,960]{1,0:T(8,128)(2,1)}, bf16[240,512]{1,0:T(8,128)(2,1)}) async-done(((bf16[240,2560]{1,0:T(8,128)(2,1)}, bf16[320,960]{1,0:T(8,128)(2,1)}, bf16[240,512]{1,0:T(8,128)(2,1)}), (bf16[240,2560]{1,0:T(8,128)(2,1)}, bf16[320,960]{1,0:T(8,128)(2,1)}, bf16[240,512]{1,0:T(8,128)(2,1)})) %all-reduce.4.cloned.1.call-update) | async-done | bytes 2088976 | tf_op jit(solution)/shard_map/psum | solution.py:804
  435.5 3.8 collective-permute-start.35
  459.0 6.3 %collective-permute-done.37.refs_2_ = bf16[64,832]{1,0:T(8,128)(2,1)} collective-permute-done((bf16[64,832]{1,0:T(8,128)(2,1)S(1)}, bf16[64,832]{1,0:T(8,128)(2,1)}, u32[]{:S(2)}, u32[]{:S(2)}) %collective-permute-start.37) | collective-permute-done | bytes 106528 | tf_op jit(solution)/shard_map/ppermute | solution.py:590
  470.1 5.3 %shard_map.219 = (f32[240,2560]{1,0:T(8,128)}, f32[240,2560]{1,0:T(8,128)}, f32[640,960]{1,0:T(8,128)}, f32[240,960]{1,0:T(8,128)}) custom-call(s32[17]{0:T(128)S(1)} %copy-done.16, bf16[240,2560]{1,0:T(8,128)(2,1)S(1)} %copy-done.3, bf16[240,2560]{1,0:T(8,128)(2,1)S(1)} %collective-permute-done.45.gut_ref, bf16[320,960]{1,0:T(8,128)(2,1)} %get-tuple-element.154.dm_ref, ...), custom_call_target="tpu_custom_call" | custom-call | bytes 12472388 | tf_op jit(solution)/shard_map/pallas_call | solution.py:46
  (258 shorter events, 154.4 us)
Async XLA Ops:
  7.2 426.9 %all-reduce.4.cloned.1.call-start = ((), (), s32[]{:S(2)}) async-start(), calls=%async_computation | async-start | bytes 4259840 | tf_op jit(solution)/shard_map/psum | solution.py:804
  37.7 18.9 %collective-permute-start.7 = (bf16[240,960]{1,0:T(8,128)(2,1)S(1)}, bf16[240,960]{1,0:T(8,128)(2,1)}, u32[]{:S(2)}, u32[]{:S(2)}) collective-permute-start(bf16[240,960]{1,0:T(8,128)(2,1)S(1)} %get-tuple-element.165.refs_0_), channel_id=1, source_target_pairs={{0,8},{1,17},{2,10},{3,19},{4,12},{5,21},{6,14},{7,23},{8,0},{9,25... | collective-permute-start | bytes 1382408 | tf_op jit(solution)/shard_map/ppermute | solution.py:590
  45.6 31.0 %collective-permute-start.16 = (bf16[240,2560]{1,0:T(8,128)(2,1)}, bf16[240,2560]{1,0:T(8,128)(2,1)}, u32[]{:S(2)}, u32[]{:S(2)}) collective-permute-start(bf16[240,2560]{1,0:T(8,128)(2,1)} %get-tuple-element.88.refs_0_), channel_id=1, source_target_pairs={{0,8},{1,17},{2,10},{3,19},{4,12},{5,21},{6,14},{7,23},{8,0},{9,25... | collective-permute-start | bytes 3686408 | tf_op jit(solution)/shard_map/ppermute | solution.py:590
  51.4 19.6 %collective-permute-start.14 = (bf16[512,640]{1,0:T(8,128)(2,1)}, bf16[512,640]{1,0:T(8,128)(2,1)}, u32[]{:S(2)}, u32[]{:S(2)}) collective-permute-start(bf16[512,640]{1,0:T(8,128)(2,1)} %collective-permute-done.13.kv_ref.refs_7_), channel_id=1, source_target_pairs={{0,2},{1,3},{2,4},{3,5},{4,6},{5,7},{8,10},{9,11},{10,12},{11,13},... | collective-permute-start | bytes 1966088 | tf_op jit(solution)/shard_map/ppermute | solution.py:590
  70.9 31.5 %collective-permute-start.15 = (bf16[512,640]{1,0:T(8,128)(2,1)}, bf16[512,640]{1,0:T(8,128)(2,1)}, u32[]{:S(2)}, u32[]{:S(2)}) collective-permute-start(bf16[512,640]{1,0:T(8,128)(2,1)} %collective-permute-done.14.kv_ref.refs_7_), channel_id=1, source_target_pairs={{0,2},{1,3},{2,4},{3,5},{4,6},{5,7},{8,10},{9,11},{10,12},{11,13},... | collective-permute-start | bytes 1966088 | tf_op jit(solution)/shard_map/ppermute | solution.py:590
  75.6 37.8 %collective-permute-start.23 = (bf16[2,256,960]{1,2,0:T(8,128)(2,1)}, bf16[2,256,960]{1,2,0:T(8,128)(2,1)}, u32[]{:S(2)}, u32[]{:S(2)}) collective-permute-start(bf16[2,256,960]{1,2,0:T(8,128)(2,1)} %param.22), channel_id=1, source_target_pairs={{0,1},{1,0},{2,3},{3,2},{4,5},{5,4},{6,7},{7,6},{8,9},{9,8},{10,11... | collective-permute-start | bytes 2949128 | tf_op jit(solution)/shard_map/ppermute | solution.py:590
  75.6 54.8 %collective-permute-start.17 = (bf16[240,2560]{1,0:T(8,128)(2,1)}, bf16[240,2560]{1,0:T(8,128)(2,1)}, u32[]{:S(2)}, u32[]{:S(2)}) collective-permute-start(bf16[240,2560]{1,0:T(8,128)(2,1)} %get-tuple-element.88.refs_0_), channel_id=1, source_target_pairs={{0,16},{1,9},{2,18},{3,11},{4,20},{5,13},{6,22},{7,15},{8,24},{9,1... | collective-permute-start | bytes 3686408 | tf_op jit(solution)/shard_map/ppermute | solution.py:590
  76.6 35.8 %collective-permute-start.19 = (bf16[320,960]{1,0:T(8,128)(2,1)}, bf16[320,960]{1,0:T(8,128)(2,1)}, u32[]{:S(2)}, u32[]{:S(2)}) collective-permute-start(bf16[320,960]{1,0:T(8,128)(2,1)} %get-tuple-element.89.refs_4_), channel_id=1, source_target_pairs={{0,8},{1,17},{2,10},{3,19},{4,12},{5,21},{6,14},{7,23},{8,0},{9,25... | collective-permute-start | bytes 1843208 | tf_op jit(solution)/shard_map/ppermute | solution.py:590
  78.1 52.3 %collective-permute-start.18 = (bf16[240,2560]{1,0:T(8,128)(2,1)}, bf16[240,2560]{1,0:T(8,128)(2,1)}, u32[]{:S(2)}, u32[]{:S(2)}) collective-permute-start(bf16[240,2560]{1,0:T(8,128)(2,1)} %collective-permute-done.16.refs_1_), channel_id=1, source_target_pairs={{0,16},{1,9},{2,18},{3,11},{4,20},{5,13},{6,22},{7,15},{8,24},{9,1... | collective-permute-start | bytes 3686408 | tf_op jit(solution)/shard_map/ppermute | solution.py:590
  166.8 22.6 %collective-permute-start.24 = (bf16[512,1920]{1,0:T(8,128)(2,1)}, bf16[512,1920]{1,0:T(8,128)(2,1)}, u32[]{:S(2)}, u32[]{:S(2)}) collective-permute-start(bf16[512,1920]{1,0:T(8,128)(2,1)} %get-tuple-element.93), channel_id=1, source_target_pairs={{0,1},{1,0},{2,3},{3,2},{4,5},{5,4},{6,7},{7,6},{8,9},{9,8},{10,11... | collective-permute-start | bytes 5898248 | tf_op jit(solution)/shard_map/ppermute | solution.py:590
  168.0 64.0 %collective-permute-start.43 = (bf16[2,240,2560]{2,1,0:T(8,128)(2,1)}, bf16[2,240,2560]{2,1,0:T(8,128)(2,1)}, u32[]{:S(2)}, u32[]{:S(2)}) collective-permute-start(bf16[2,240,2560]{2,1,0:T(8,128)(2,1)} %get-tuple-element.121), channel_id=1, source_target_pairs={{0,16},{1,9},{2,18},{3,11},{4,20},{5,13},{6,22},{7,15},{8,24},{9,1... | collective-permute-start | bytes 7372808 | tf_op jit(solution)/shard_map/ppermute | solution.py:590
  188.8 132.5 %collective-permute-start.47 = (bf16[320,960]{1,0:T(8,128)(2,1)}, bf16[320,960]{1,0:T(8,128)(2,1)}, u32[]{:S(2)}, u32[]{:S(2)}) collective-permute-start(bf16[320,960]{1,0:T(8,128)(2,1)} %slice_bitcast_fusion.2), channel_id=1, source_target_pairs={{0,8},{1,17},{2,10},{3,19},{4,12},{5,21},{6,14},{7,23},{8,0},{9,25... | collective-permute-start | bytes 1843208 | tf_op jit(solution)/shard_map/ppermute | solution.py:590
  200.4 33.9 %collective-permute-start.49 = (bf16[4,240,512]{2,1,0:T(8,128)(2,1)S(1)}, bf16[4,240,512]{2,1,0:T(8,128)(2,1)S(1)}, u32[]{:S(2)}, u32[]{:S(2)}) collective-permute-start(bf16[4,240,512]{2,1,0:T(8,128)(2,1)S(1)} %get-tuple-element.125), channel_id=1, source_target_pairs={{0,1},{1,0},{2,3},{3,2},{4,5},{5,4},{6,7},{7,6},{8,9},{9,8},{10,11... | collective-permute-start | bytes 2949128 | tf_op jit(solution)/shard_map/ppermute | solution.py:590
  204.2 26.3 %collective-permute-start.26 = (bf16[512,640]{1,0:T(8,128)(2,1)S(1)}, bf16[512,640]{1,0:T(8,128)(2,1)S(1)}, u32[]{:S(2)}, u32[]{:S(2)}) collective-permute-start(bf16[512,640]{1,0:T(8,128)(2,1)S(1)} %get-tuple-element.109), channel_id=1, source_target_pairs={{2,0},{3,1},{4,2},{5,3},{6,4},{7,5},{10,8},{11,9},{12,10},{13,11},... | collective-permute-start | bytes 1966088 | tf_op jit(solution)/shard_map/ppermute | solution.py:590
  230.7 35.5 %collective-permute-start.27 = (bf16[512,640]{1,0:T(8,128)(2,1)S(1)}, bf16[512,640]{1,0:T(8,128)(2,1)S(1)}, u32[]{:S(2)}, u32[]{:S(2)}) collective-permute-start(bf16[512,640]{1,0:T(8,128)(2,1)S(1)} %add_convert_fusion.6), channel_id=1, source_target_pairs={{2,0},{3,1},{4,2},{5,3},{6,4},{7,5},{10,8},{11,9},{12,10},{13,11},... | collective-permute-start | bytes 1966088 | tf_op jit(solution)/shard_map/ppermute | solution.py:590
  235.7 82.8 %collective-permute-start.50 = (bf16[2,240,512]{2,1,0:T(8,128)(2,1)}, bf16[2,240,512]{2,1,0:T(8,128)(2,1)}, u32[]{:S(2)}, u32[]{:S(2)}) collective-permute-start(bf16[2,240,512]{2,1,0:T(8,128)(2,1)} %slice.75), channel_id=1, source_target_pairs={{0,16},{1,9},{2,18},{3,11},{4,20},{5,13},{6,22},{7,15},{8,24},{9,1... | collective-permute-start | bytes 1474568 | tf_op jit(solution)/shard_map/ppermute | solution.py:590
  266.3 37.8 %collective-permute-start.28 = (bf16[512,640]{1,0:T(8,128)(2,1)S(1)}, bf16[512,640]{1,0:T(8,128)(2,1)S(1)}, u32[]{:S(2)}, u32[]{:S(2)}) collective-permute-start(bf16[512,640]{1,0:T(8,128)(2,1)S(1)} %add_convert_fusion.5), channel_id=1, source_target_pairs={{2,0},{3,1},{4,2},{5,3},{6,4},{7,5},{10,8},{11,9},{12,10},{13,11},... | collective-permute-start | bytes 1966088 | tf_op jit(solution)/shard_map/ppermute | solution.py:590
  268.9 58.0 %collective-permute-start.44 = (bf16[240,2560]{1,0:T(8,128)(2,1)}, bf16[240,2560]{1,0:T(8,128)(2,1)}, u32[]{:S(2)}, u32[]{:S(2)}) collective-permute-start(bf16[240,2560]{1,0:T(8,128)(2,1)} %slice_bitcast_fusion), channel_id=1, source_target_pairs={{0,8},{1,17},{2,10},{3,19},{4,12},{5,21},{6,14},{7,23},{8,0},{9,25... | collective-permute-start | bytes 3686408 | tf_op jit(solution)/shard_map/ppermute | solution.py:590
  355.8 78.3 %collective-permute-start.32 = (bf16[256,832]{1,0:T(8,128)(2,1)}, bf16[256,832]{1,0:T(8,128)(2,1)}, u32[]{:S(2)}, u32[]{:S(2)}) collective-permute-start(bf16[256,832]{1,0:T(8,128)(2,1)} %slice_bitcast_fusion.4), channel_id=1, source_target_pairs={{0,8},{1,17},{2,10},{3,19},{4,12},{5,21},{6,14},{7,23},{8,0},{9,25... | collective-permute-start | bytes 1277960 | tf_op jit(solution)/shard_map/ppermute | solution.py:590
  358.6 80.7 %collective-permute-start.25 = (bf16[256,960]{1,0:T(8,128)(2,1)}, bf16[256,960]{1,0:T(8,128)(2,1)}, u32[]{:S(2)}, u32[]{:S(2)}) collective-permute-start(bf16[256,960]{1,0:T(8,128)(2,1)} %constant_dynamic-slice_fusion.4), channel_id=1, source_target_pairs={{0,1},{1,0},{2,3},{3,2},{4,5},{5,4},{6,7},{7,6},{8,9},{9,8},{10,11... | collective-permute-start | bytes 1474568 | tf_op jit(solution)/shard_map/ppermute | solution.py:590
  359.4 96.0 %collective-permute-start.29 = (bf16[256,960]{1,0:T(8,128)(2,1)}, bf16[256,960]{1,0:T(8,128)(2,1)}, u32[]{:S(2)}, u32[]{:S(2)}) collective-permute-start(bf16[256,960]{1,0:T(8,128)(2,1)} %constant_dynamic-slice_fusion.3), channel_id=1, source_target_pairs={{0,1},{1,0},{2,3},{3,2},{4,5},{5,4},{6,7},{7,6},{8,9},{9,8},{10,11... | collective-permute-start | bytes 1474568 | tf_op jit(solution)/shard_map/ppermute | solution.py:590
  434.1 35.0 %collective-permute-start.45 = (bf16[240,2560]{1,0:T(8,128)(2,1)}, bf16[240,2560]{1,0:T(8,128)(2,1)S(1)}, u32[]{:S(2)}, u32[]{:S(2)}) collective-permute-start(bf16[240,2560]{1,0:T(8,128)(2,1)} %get-tuple-element.153.gum_ref), channel_id=1, source_target_pairs={{0,1},{1,0},{2,3},{3,2},{4,5},{5,4},{6,7},{7,6},{8,9},{9,8},{10,11... | collective-permute-start | bytes 3686408 | tf_op jit(solution)/shard_map/ppermute | solution.py:590
  458.2 20.4 %collective-permute-start.39 = (bf16[64,832]{1,0:T(8,128)(2,1)S(1)}, bf16[64,832]{1,0:T(8,128)(2,1)S(1)}, u32[]{:S(2)}, u32[]{:S(2)}) collective-permute-start(bf16[64,832]{1,0:T(8,128)(2,1)S(1)} %add_convert_fusion.8.refs_0_), channel_id=1, source_target_pairs={{0,1},{1,0},{2,3},{3,2},{4,5},{5,4},{6,7},{7,6},{8,9},{9,8},{10,11... | collective-permute-start | bytes 319496 | tf_op jit(solution)/shard_map/ppermute | solution.py:590
  459.0 19.6 %collective-permute-start.42 = (bf16[64,832]{1,0:T(8,128)(2,1)S(1)}, bf16[64,832]{1,0:T(8,128)(2,1)}, u32[]{:S(2)}, u32[]{:S(2)}) collective-permute-start(bf16[64,832]{1,0:T(8,128)(2,1)S(1)} %collective-permute-done.38.refs_3_), channel_id=1, source_target_pairs={{0,1},{1,0},{2,3},{3,2},{4,5},{5,4},{6,7},{7,6},{8,9},{9,8},{10,11... | collective-permute-start | bytes 319496 | tf_op jit(solution)/shard_map/ppermute | solution.py:590
  (76 other events, 935.7 us)
Sparse Core Ops, SparseCore 0:
  329.7 104.3 all-reduce.3

commit v2 on v1

v2 whole, which is shorter than its diff:
```python
import functools

import jax
import jax.numpy as jnp
from jax import lax
from jax.experimental import pallas as pl
from jax.experimental.pallas import tpu as pltpu
from jax.sharding import PartitionSpec as P

QUERY_HEAD_COUNT = 15
KEY_HEAD_COUNT = 5
HEAD_DIM = 64
GROUP = QUERY_HEAD_COUNT // KEY_HEAD_COUNT

eps_norm = 1e-05
rope_base = 100000.0
masked_score = -1e30

f32 = jnp.float32
bf16 = jnp.bfloat16
AXES = ("fsdp", "ctx")
SMALL = 32 * 1024 * 1024
LARGE = 60 * 1024 * 1024

NN = ((1,), (0,))
NT = ((1,), (1,))
TN = ((0,), (0,))


def dot(a, b, dims=NN):
    return lax.dot_general(a, b, (dims, ((), ())), preferred_element_type=f32)


def call(kernel, outs, args, micros, scratch=(), smem=0, hbm=(), outs_hbm=(), after=(), vmem=SMALL):
    count = len(args)
    specs = []
    for k in range(count):
        if k < smem:
            specs.append(pl.BlockSpec(memory_space=pltpu.SMEM))
        elif k in hbm:
            specs.append(pl.BlockSpec(memory_space=pl.ANY))
        else:
            specs.append(pl.BlockSpec(memory_space=pltpu.VMEM))
    specs += [pl.BlockSpec(memory_space=pl.ANY)] * len(after)
    shapes = [jax.ShapeDtypeStruct(s, d) for s, d in outs]

    def body(*refs):
        kernel(*refs[:count], *refs[count + len(after) :])

    return pl.pallas_call(
        body,
        out_shape=shapes,
        in_specs=specs,
        out_specs=[
            pl.BlockSpec(memory_space=pl.ANY if k in outs_hbm else pltpu.VMEM)
            for k in range(len(shapes))
        ],
        scratch_shapes=list(scratch),
        compiler_params=pltpu.CompilerParams(vmem_limit_bytes=vmem),
        cost_estimate=pl.CostEstimate(
            flops=int(micros * 1.15e9), bytes_accessed=0, transcendentals=0
        ),
    )(*args, *after)


def call_grid(kernel, steps, outs, args, micros, scratch=(), after=(), vmem=SMALL):
    scalars, args = args[0], args[1:]
    count = len(args)

    def body(*refs):
        kernel(*refs[: count + 1], *refs[count + 1 + len(after) :])

    return pl.pallas_call(
        body,
        out_shape=[jax.ShapeDtypeStruct(shape, kind) for (shape, kind), _, _ in outs],
        grid_spec=pltpu.PrefetchScalarGridSpec(
            num_scalar_prefetch=1,
            grid=(steps,),
            in_specs=[pl.BlockSpec(block, index) for _, block, index in args]
            + [pl.BlockSpec(memory_space=pl.ANY)] * len(after),
            out_specs=[pl.BlockSpec(block, index) for _, block, index in outs],
            scratch_shapes=list(scratch),
        ),
        compiler_params=pltpu.CompilerParams(
            dimension_semantics=("arbitrary",), vmem_limit_bytes=vmem
        ),
        cost_estimate=pl.CostEstimate(
            flops=int(micros * 1.15e9), bytes_accessed=0, transcendentals=0
        ),
    )(scalars, *[a for a, _, _ in args], *after)


def whole(array):
    rank = len(array.shape)
    return (array, array.shape, lambda i, s: (0,) * rank)


def leading(array, size):
    rank = len(array.shape)
    return (array, (size, *array.shape[1:]), lambda i, s: (i,) + (0,) * (rank - 1))


def trailing(array, size):
    rank = len(array.shape)
    return (array, (*array.shape[:-1], size), lambda i, s: (0,) * (rank - 1) + (i,))


class Out:
    def __init__(self, shape, kind):
        self.shape, self.kind = shape, kind

    def __iter__(self):
        return iter((self.shape, self.kind))


def rotate_rows(part, cos, sin):
    half = HEAD_DIM // 2
    a, b = part[:half], part[half:]
    return jnp.concatenate([a * cos - b * sin, b * cos + a * sin], axis=0)


def unrotate_rows(part, cos, sin):
    half = HEAD_DIM // 2
    a, b = part[:half], part[half:]
    return jnp.concatenate([a * cos + b * sin, b * cos - a * sin], axis=0)


def run_copies(pairs, sems):
    copies = [pltpu.make_async_copy(a, b, sems.at[k]) for k, (a, b) in enumerate(pairs)]
    for copy in copies:
        copy.start()
    return copies


def placed(pieces, dst, order_ref, base, rows):
    pairs = []
    for s, piece in enumerate(pieces):
        if len(pieces) == 1:
            pairs.append((piece, dst))
        else:
            at = pl.multiple_of(order_ref[base + s] * rows, 16)
            pairs.append((piece.at[pl.ds(0, rows)], dst.at[pl.ds(at, rows)]))
    return pairs


def inverse_norm(field):
    return lax.rsqrt(jnp.mean(field * field, axis=0, keepdims=True) + eps_norm)


def norm_back(grad_normed, field, inverse, scale_gain):
    scaled = grad_normed * scale_gain
    gain_term = jnp.sum(grad_normed * field * inverse, axis=1, keepdims=True)
    grad_field = inverse * scaled - field * (inverse * inverse * inverse) * jnp.mean(
        scaled * field, axis=0, keepdims=True
    )
    return grad_field, gain_term


def first_kernel(order_ref, x_ref, k_ref, v_ref, gain_ref, item_ref, send_ref, sem):
    core = order_ref[0]
    copy = pltpu.make_async_copy(x_ref.at[1 - core], send_ref, sem)
    copy.start()
    wide = k_ref.shape[0]

    @pl.when(core == 0)
    def _():
        item_ref[:wide, :] = k_ref[...]

    @pl.when(core == 1)
    def _():
        item_ref[:wide, :] = v_ref[...]

    item_ref[wide:, :] = gain_ref[...]
    copy.wait()


def key_kernel(parts, slots, order_ref, x_ref, got_ref, cos_ref, sin_ref, *refs):
    mine, theirs = refs[:parts], refs[parts : 2 * parts]
    xt_ref, n1t_ref, kv_ref, w_ref, gain_ref, sems = refs[2 * parts :]
    core = order_ref[0]
    width, tokens = xt_ref.shape
    rows = width // parts
    half = tokens // 2
    pairs = [
        (x_ref.at[core], xt_ref.at[:, pl.ds(pl.multiple_of(core * half, 128), half)]),
        (got_ref, xt_ref.at[:, pl.ds(pl.multiple_of((1 - core) * half, 128), half)]),
    ]
    for s in range(parts):
        j = order_ref[1 + core * slots + s] if parts > 1 else 0
        pairs.append((mine[s], w_ref.at[core, j]))
    for s in range(parts):
        j = order_ref[1 + (1 - core) * slots + s] if parts > 1 else 0
        pairs.append((theirs[s], w_ref.at[1 - core, j]))
    copies = run_copies(pairs, sems)
    for copy in copies:
        copy.wait()
    x = xt_ref[...].astype(f32)
    inv = inverse_norm(x)
    kv_width = KEY_HEAD_COUNT * HEAD_DIM
    for j in range(parts):
        gain_ref[rows * j : rows * (j + 1), :] = w_ref[0, j, kv_width:, :].astype(f32).T[:, :8]
    n1t_ref[...] = (x * inv * gain_ref[:, 0:1]).astype(bf16)
    cos, sin = cos_ref[...], sin_ref[...]
    lin = []
    for c in range(2):
        total = None
        for j in range(parts):
            more = dot(w_ref[c, j, :kv_width, :], n1t_ref[rows * j : rows * (j + 1), :])
            total = more if total is None else total + more
        lin.append(total)
    turned = [
        rotate_rows(lin[0][HEAD_DIM * h : HEAD_DIM * (h + 1)], cos, sin)
        for h in range(KEY_HEAD_COUNT)
    ]
    kv_ref[...] = jnp.concatenate(turned + [lin[1]], axis=0).T.astype(bf16)


def query_kernel(parts, slots, order_ref, n1t_ref, cos_ref, sin_ref, *refs):
    mine, theirs = refs[:parts], refs[parts : 2 * parts]
    qt_ref, q_ref, wq_ref, wo_ref, sems = refs[2 * parts :]
    core = order_ref[0]
    rows = n1t_ref.shape[0] // parts

    for c in range(2):

        @pl.when(core == c)
        def _():
            mine_to, theirs_to = (wq_ref, wo_ref) if c == 0 else (wo_ref, wq_ref)
            pairs = placed(mine, mine_to, order_ref, 1 + c * slots, rows)
            pairs += placed(theirs, theirs_to, order_ref, 1 + (1 - c) * slots, rows)
            for copy in run_copies(pairs, sems):
                copy.wait()

    cos, sin = cos_ref[...], sin_ref[...]
    lin_t = dot(wq_ref[...], n1t_ref[...], TN)
    for h in range(QUERY_HEAD_COUNT):
        turned = rotate_rows(lin_t[HEAD_DIM * h : HEAD_DIM * (h + 1)], cos, sin) * 0.125
        qt_ref[h] = turned.astype(bf16)
        q_ref[h] = turned.T.astype(bf16)


def pack_down(block, rows):
    rest = block.shape[0] - rows
    count = rows // rest
    cols = block.shape[1] // count
    extra = [block[rows:, cols * k : cols * (k + 1)] for k in range(count)]
    return jnp.concatenate([block[:rows], jnp.concatenate(extra, axis=0)], axis=1)


def unpack_down(packed, width):
    rows = packed.shape[0]
    cols = packed.shape[1] - width
    count = width // cols
    rest = rows // count
    extra = [packed[rest * k : rest * (k + 1), width:] for k in range(count)]
    return jnp.concatenate([packed[:, :width], jnp.concatenate(extra, axis=1)], axis=0)


def halves_kernel(slots, order_ref, q_ref, o_ref, gate_ref, up_ref, down_ref, qo_ref, gu_ref, d_ref):
    ff = gate_ref.shape[1]
    step = ff // slots
    half = step // 2
    for c in range(2):

        @pl.when(order_ref[0] == c)
        def _():
            qo_ref[...] = q_ref[...] if c == 0 else o_ref[...]
            for j in range(slots):
                src = slice(step * j + half * c, step * j + half * (c + 1))
                gu_ref[:, half * j : half * (j + 1)] = gate_ref[:, src]
                gu_ref[:, ff // 2 + half * j : ff // 2 + half * (j + 1)] = up_ref[:, src]
            d_ref[...] = down_ref[:, half * c : half * (c + 1)].astype(f32).T.astype(bf16)


def split_values(kv_ref, k_scr, vt_scr):
    for g in range(KEY_HEAD_COUNT):
        k_scr[g] = kv_ref[:, HEAD_DIM * g : HEAD_DIM * (g + 1)]
        start = HEAD_DIM * (KEY_HEAD_COUNT + g)
        vt_scr[g] = kv_ref[:, start : start + HEAD_DIM].astype(f32).T.astype(bf16)


def forward_diagonal(ok_ref, qt_ref, kv_ref, m_ref, l_ref, acc_ref, k_scr, vt_scr):
    g = pl.program_id(0)

    @pl.when(g == 0)
    def _():
        split_values(kv_ref, k_scr, vt_scr)

    half = kv_ref.shape[0] // 2
    m_ref[...] = jnp.zeros_like(m_ref)
    l_ref[...] = jnp.ones_like(l_ref)
    for i in range(GROUP):
        for part in range(2):
            cols = slice(part * half, (part + 1) * half)
            used = (part + 1) * half
            st = dot(k_scr[g, :used, :], qt_ref[i, :, cols])
            key_at = lax.broadcasted_iota(jnp.int32, st.shape, 0)
            row_at = lax.broadcasted_iota(jnp.int32, st.shape, 1) + part * half
            st = jnp.where(key_at <= row_at, st, masked_score)
            top = jnp.max(st, axis=0, keepdims=True)
            p = jnp.exp(st - top)
            m_ref[0, i : i + 1, cols] = top
            l_ref[0, i : i + 1, cols] = jnp.sum(p, axis=0, keepdims=True)
            acc_ref[i, :, cols] = dot(vt_scr[g, :, :used], p.astype(bf16))


def forward_full(
    ok_ref, qt_ref, kv_ref, m_in, l_in, acc_in, m_ref, l_ref, acc_ref, k_scr, vt_scr
):
    g = pl.program_id(0)
    m_ref[...] = m_in[...]
    l_ref[...] = l_in[...]

    @pl.when(ok_ref[0] == 0)
    def _():
        acc_ref[...] = acc_in[...]

    @pl.when(ok_ref[0] != 0)
    def _():
        @pl.when(g == 0)
        def _():
            split_values(kv_ref, k_scr, vt_scr)

        for i in range(GROUP):
            st = dot(k_scr[g], qt_ref[i])
            old = m_in[0, i : i + 1, :]
            top = jnp.maximum(old, jnp.max(st, axis=0, keepdims=True))
            factor = jnp.exp(old - top)
            p = jnp.exp(st - top)
            m_ref[0, i : i + 1, :] = top
            l_ref[0, i : i + 1, :] = l_in[0, i : i + 1, :] * factor + jnp.sum(
                p, axis=0, keepdims=True
            )
            acc_ref[i] = acc_in[i] * factor + dot(vt_scr[g], p.astype(bf16))


def middle_kernel(xt_ref, acc_ref, l_ref, wo_ref, gain_ref, att_ref, mid_ref, n2_ref):
    for h in range(QUERY_HEAD_COUNT):
        g, i = divmod(h, GROUP)
        att_ref[HEAD_DIM * h : HEAD_DIM * (h + 1), :] = (
            acc_ref[h] / l_ref[g, i : i + 1, :]
        ).astype(bf16)
    middle = xt_ref[...].astype(f32) + dot(wo_ref[...], att_ref[...], TN)
    mid_ref[...] = middle
    n2_ref[...] = (middle * inverse_norm(middle) * gain_ref[:, 1:2]).astype(bf16)


def place_cotangent(order_ref, own_ref, got_ref, dst, both):
    core = order_ref[0]
    half = own_ref.shape[2]
    pairs = []
    for k in range(2 if both else 1):
        seq = core if k == 0 else 1 - core
        for ref, at in ((own_ref, core), (got_ref, 1 - core)):
            start = pl.multiple_of(2 * half * k + at * half, 128)
            pairs.append((ref.at[seq], dst.at[:, pl.ds(start, half)]))
    return pairs


def ff_kernel(parts, slots, groups, tile, order_ref, gu_ref, *refs):
    d_pieces, refs = refs[:parts], refs[parts:]
    n2m_ref, n2t_ref, own_ref, got_ref, out_ref, gn_ref, send_ref = refs[:7]
    refs = refs[7:]
    outs = refs[:groups]
    w, wd, n2, n2_t, cot, cot_t, out, gn, grads, gd, sems, out_sems = refs[groups:]
    core = order_ref[0]
    width, ff2 = w.shape
    ff = ff2 // 2
    rows = n2m_ref.shape[1]
    base = 1 + core * slots
    pairs = place_cotangent(order_ref, own_ref, got_ref, cot_t, True)
    pairs.append((n2m_ref, n2_t.at[:, pl.ds(0, rows)]))
    pairs.append((n2t_ref, n2_t.at[:, pl.ds(rows, rows)]))
    early = len(pairs)
    pairs += placed(d_pieces, wd, order_ref, base, ff // parts)
    pairs.append((gu_ref, w))
    copies = run_copies(pairs, sems)
    for copy in copies[:early]:
        copy.wait()
    cot[...] = cot_t[...].T
    n2[...] = n2_t[...].T
    out[...] = jnp.zeros_like(out)
    gn[...] = jnp.zeros_like(gn)
    for copy in copies[early:]:
        copy.wait()
    shard = width // slots

    @pl.loop(0, ff // tile)
    def _(step):
        at = pl.multiple_of(step * tile, tile)
        up_at = pl.multiple_of(ff + step * tile, 128)
        wg = w[:, pl.ds(at, tile)]
        wu = w[:, pl.ds(up_at, tile)]
        w_down = wd[pl.ds(at, tile), :]
        gate = dot(n2[...], wg)
        up = dot(n2[...], wu)
        s = jax.nn.sigmoid(gate)
        swish = gate * s
        hidden = (swish * up).astype(bf16)
        grad_hidden = dot(cot[...], w_down, NT)
        grad_gate = (grad_hidden * up * s * (1.0 + gate * (1.0 - s))).astype(bf16)
        grad_up = (grad_hidden * swish).astype(bf16)
        out[...] += dot(hidden, w_down)
        gn[...] += dot(grad_gate, wg, NT) + dot(grad_up, wu, NT)
        gd[pl.ds(at, tile), :] = dot(hidden, cot[...], TN).astype(bf16)
        g_gate = dot(n2_t[...], grad_gate).astype(bf16)
        g_up = dot(n2_t[...], grad_up).astype(bf16)
        for j in range(slots):
            slot = order_ref[1 + (2 + core) * slots + j]
            grads[slot, :, pl.ds(at, tile)] = g_gate[shard * j : shard * (j + 1)]
            grads[slot, :, pl.ds(up_at, tile)] = g_up[shard * j : shard * (j + 1)]

    per = slots // groups
    down_rows = ff // slots
    for j in range(slots):
        slot = order_ref[1 + (2 + core) * slots + j]
        rows_j = gd[down_rows * j : down_rows * (j + 1), :].astype(f32)
        grads[slot, :, ff2:] = pack_down(rows_j, shard).astype(bf16)
    copies = run_copies(
        [(grads.at[pl.ds(per * k, per)], outs[k]) for k in reversed(range(groups))], out_sems
    )
    out_ref[...] = out[:rows, :].T
    gn_ref[...] = gn[:rows, :].T
    send_ref[:width, :] = out[rows:, :].T.astype(bf16)
    send_ref[width:, :] = gn[rows:, :].T.astype(bf16)
    for copy in copies:
        copy.wait()


def spread(slots, order_ref, part, core, piece, keep_ref, send_ref):
    shard, wide = keep_ref.shape[1], piece.shape[1]
    for keep in range(2):
        ref = keep_ref if keep else send_ref

        @pl.when((core == part) == (keep == 1))
        def _():
            if wide < ref.shape[2]:
                ref[:, :, wide:] = jnp.zeros((slots, shard, ref.shape[2] - wide), bf16)
            for j in range(slots):
                slot = order_ref[1 + (2 + part) * slots + j]
                ref[slot, :, :wide] = piece[shard * j : shard * (j + 1)].astype(bf16)


def turn_kernel(
    slots, order_ref, mid_ref, sum_ref, gn_ref, got_ref, gain_ref, own_cot_ref, got_cot_ref, wo_ref,
    att_ref, acc_ref, m_ref, l_ref,
    fin_ref, gm_ref, og_ref, og_send_ref, do_ref, dot_ref, del_ref, lse_ref, gg_ref, og, gains,
):
    core = order_ref[0]
    step, last = pl.program_id(0), pl.num_programs(0) - 1
    middle = mid_ref[...]
    width = middle.shape[0]
    fin_ref[...] = (middle + sum_ref[...] + got_ref[:width, :].astype(f32)).astype(bf16)
    gn = gn_ref[...] + got_ref[width:, :].astype(f32)
    grad_field, gain_term = norm_back(gn, middle, inverse_norm(middle), gain_ref[:, 1:2])
    gm = jnp.where(step == core, own_cot_ref[0], got_cot_ref[0]).astype(f32) + grad_field
    gm_ref[...] = gm
    low = gm.astype(bf16)
    more = dot(att_ref[...], low, NT)
    gain_term = jnp.broadcast_to(gain_term, gains.shape)

    @pl.when(step == 0)
    def _():
        og[...] = more
        gains[...] = gain_term

    @pl.when(step != 0)
    def _():
        og[...] += more
        gains[...] += gain_term

    ga_t = dot(wo_ref[...], low)
    del_ref[...] = jnp.zeros_like(del_ref)
    lse_ref[...] = m_ref[...] + jnp.log(l_ref[...])
    for h in range(QUERY_HEAD_COUNT):
        g, i = divmod(h, GROUP)
        part = ga_t[HEAD_DIM * h : HEAD_DIM * (h + 1)].astype(bf16)
        dot_ref[h] = part
        wide = part.astype(f32)
        do_ref[h] = wide.T.astype(bf16)
        del_ref[g, i : i + 1, :] = jnp.sum(
            wide * (acc_ref[h] / l_ref[g, i : i + 1, :]), axis=0, keepdims=True
        )

    @pl.when(step == last)
    def _():
        gg_ref[...] = gains[...]
        split = og_ref.shape[2]
        spread(slots, order_ref, 0, core, og[:, :split], og_ref, og_send_ref)
        spread(slots, order_ref, 1, core, og[:, split:], og_ref, og_send_ref)


def backward_kernel(diagonal, first, *refs):
    if first:
        ok_ref, qt_ref, q_ref, dot_ref, do_ref, lse_ref, del_ref, kv_ref, dq_ref, dkv_ref, *scr = refs
        dq_in = None
    else:
        (
            ok_ref, qt_ref, q_ref, dot_ref, do_ref, lse_ref, del_ref, kv_ref, dq_in, dq_ref, dkv_ref, *scr,
        ) = refs
    k_scr, v_scr, kt_scr, dk_scr, dv_scr = scr
    keys = kv_ref.shape[0]
    g = pl.program_id(0)

    @pl.when(ok_ref[0] == 0)
    def _():
        dq_ref[...] = jnp.zeros_like(dq_ref) if first else dq_in[...]
        dkv_ref[...] = jnp.zeros_like(dkv_ref)

    @pl.when(ok_ref[0] != 0)
    def _():
        @pl.when(g == 0)
        def _():
            for j in range(KEY_HEAD_COUNT):
                k = kv_ref[:, HEAD_DIM * j : HEAD_DIM * (j + 1)]
                k_scr[j] = k
                kt_scr[j] = k.astype(f32).T.astype(bf16)
                start = HEAD_DIM * (KEY_HEAD_COUNT + j)
                v_scr[j] = kv_ref[:, start : start + HEAD_DIM]

        parts = 2 if diagonal else 1
        rows = q_ref.shape[1]
        for part in range(parts):
            cols = slice(part * rows // parts, (part + 1) * rows // parts)
            used = (part + 1) * rows // parts if diagonal else keys
            dk = dv = None
            for i in range(GROUP):
                st = dot(k_scr[g, :used, :], qt_ref[i, :, cols])
                p = jnp.exp(st - lse_ref[0, i : i + 1, cols])
                if diagonal:
                    key_at = lax.broadcasted_iota(jnp.int32, st.shape, 0)
                    row_at = lax.broadcasted_iota(jnp.int32, st.shape, 1) + cols.start
                    p = jnp.where(key_at <= row_at, p, 0.0)
                dpt = dot(v_scr[g, :used, :], dot_ref[i, :, cols])
                ds = (p * (dpt - del_ref[0, i : i + 1, cols])).astype(bf16)
                more_v = dot(p.astype(bf16), do_ref[i, cols, :])
                more_k = dot(ds, q_ref[i, cols, :])
                dv = more_v if dv is None else dv + more_v
                dk = more_k if dk is None else dk + more_k
                more_q = dot(kt_scr[g, :, :used], ds)
                if first:
                    dq_ref[i, :, cols] = more_q
                else:
                    dq_ref[i, :, cols] = dq_in[i, :, cols] + more_q
            if part == 0:
                dk_scr[g, :used, :] = dk
                dv_scr[g, :used, :] = dv
            else:
                before = part * rows // parts
                dk_scr[g, :before, :] += dk[:before]
                dv_scr[g, :before, :] += dv[:before]
                dk_scr[g, before:used, :] = dk[before:]
                dv_scr[g, before:used, :] = dv[before:]

        @pl.when(g == KEY_HEAD_COUNT - 1)
        def _():
            dkv_ref[...] = jnp.concatenate(
                [dk_scr[j].astype(bf16) for j in range(KEY_HEAD_COUNT)]
                + [dv_scr[j].astype(bf16) for j in range(KEY_HEAD_COUNT)],
                axis=1,
            )


def last_kernel(
    parts, slots, order_ref, dq_ref, dkv_ref, got_ref, n1t_ref, wq_ref, w_ref, cos_ref, sin_ref,
    xt_ref, gain_ref, gm_ref, gg_two_ref,
    ig_ref, keep_ref, send_ref, dqt_scr, rhs_scr, gn_scr, one, two, gains_scr,
):
    core = order_ref[0]
    step, last = pl.program_id(0), pl.num_programs(0) - 1
    cos, sin = cos_ref[...], sin_ref[...]
    width = dqt_scr.shape[0]
    kv_width = KEY_HEAD_COUNT * HEAD_DIM
    cut = keep_ref.shape[2]
    for h in range(QUERY_HEAD_COUNT):
        at = HEAD_DIM * h
        turned = unrotate_rows(dq_ref[h] * 0.125, cos, sin).astype(bf16)
        dqt_scr[at : at + HEAD_DIM, :] = turned
        if at >= cut:
            rhs_scr[2 * kv_width + at - cut : 2 * kv_width + at - cut + HEAD_DIM, :] = turned
    dkv = (dkv_ref[...].astype(f32) + got_ref[...].astype(f32)).T
    for h in range(KEY_HEAD_COUNT):
        at = HEAD_DIM * h
        rhs_scr[at : at + HEAD_DIM, :] = unrotate_rows(dkv[at : at + HEAD_DIM], cos, sin).astype(
            bf16
        )
    rhs_scr[kv_width : 2 * kv_width, :] = dkv[kv_width:].astype(bf16)
    gn_scr[...] = dot(wq_ref[...], dqt_scr[...])
    rows = width // parts
    for j in range(parts):
        gn_scr[rows * j : rows * (j + 1), :] += dot(
            w_ref[0, j, :kv_width, :], rhs_scr[:kv_width, :], TN
        ) + dot(w_ref[1, j, :kv_width, :], rhs_scr[kv_width : 2 * kv_width, :], TN)
    x = xt_ref[...].astype(f32)
    grad_field, gg_one = norm_back(gn_scr[...], x, inverse_norm(x), gain_ref[:, 0:1])
    ig_ref[...] = (gm_ref[...] + grad_field).astype(bf16)
    more_one = dot(n1t_ref[...], dqt_scr[:cut, :], NT)
    more_two = dot(n1t_ref[...], rhs_scr[...], NT)
    gg_one = jnp.broadcast_to(gg_one, gains_scr.shape)

    @pl.when(step == 0)
    def _():
        one[...] = more_one
        two[...] = more_two
        gains_scr[...] = gg_one

    @pl.when(step != 0)
    def _():
        one[...] += more_one
        two[...] += more_two
        gains_scr[...] += gg_one

    @pl.when(step == last)
    def _():
        free = cut - two.shape[1]
        lane_at = lax.broadcasted_iota(jnp.int32, (width, free), 1)
        gains = jnp.where(
            lane_at == 0, gains_scr[:, 0:1], jnp.where(lane_at == 1, gg_two_ref[:, 0:1], 0.0)
        )
        spread(slots, order_ref, 0, core, one[...], keep_ref, send_ref)
        spread(
            slots, order_ref, 1, core, jnp.concatenate([two[...], gains], axis=1), keep_ref, send_ref
        )


def add_kernel(a_ref, b_ref, *outs):
    for k, out in enumerate(outs):
        if len(outs) == 1:
            out[...] = (a_ref[...].astype(f32) + b_ref[...].astype(f32)).astype(bf16)
        elif out.shape == a_ref.shape[1:]:
            out[...] = (a_ref[k].astype(f32) + b_ref[k].astype(f32)).astype(bf16)
        else:
            at = slice(k * out.shape[0], (k + 1) * out.shape[0])
            out[...] = (a_ref[at].astype(f32) + b_ref[at].astype(f32)).astype(bf16)


def join_kernel(*refs):
    out, refs = refs[-1], refs[:-1]
    block = out.shape[1]
    rows = refs[0].shape[0]
    at = 0
    for a_ref, b_ref in zip(refs[0::2], refs[1::2]):
        cols = a_ref.shape[1]
        total = a_ref[...].astype(f32) + b_ref[...].astype(f32)
        for k in range(out.shape[0]):
            used = max(0, min(block, rows - block * k))
            if used > 0:
                out[k, :used, at : at + cols] = total[block * k : block * k + used].astype(bf16)
            if used < block:
                out[k, used:, at : at + cols] = jnp.zeros((block - used, cols), bf16)
        at += cols


def add_pieces_kernel(chips, order_ref, a_ref, b_ref, *refs):
    outs, scr = refs[:chips], refs[chips]
    step = outs[0].shape[0]
    rows = a_ref.shape[0]
    scr[:rows, :] = a_ref[...].astype(f32) + b_ref[...].astype(f32)
    if rows < scr.shape[0]:
        scr[rows:, :] = jnp.zeros((scr.shape[0] - rows, scr.shape[1]), f32)
    for k in range(chips):
        at = pl.multiple_of(lax.rem(order_ref[1] + k, chips) * step, 16)
        outs[k][...] = scr[pl.ds(at, step), :].astype(bf16)


def sum_kernel(*refs):
    total = refs[0][...].astype(f32)
    for ref in refs[1:-1]:
        total = total + ref[...].astype(f32)
    refs[-1][...] = total.astype(bf16)


def finish_ff_kernel(slots, got_ref, gate_ref, up_ref, down_ref, o_ref, scr):
    shard, ff = gate_ref.shape
    step = ff // slots
    half = step // 2
    width = o_ref.shape[1]
    chips, block = got_ref.shape[0] // 2, got_ref.shape[1]
    packed = ff + ff // 2
    split = got_ref.shape[2] - packed
    for c in range(2):
        for k in range(chips):
            used = max(0, min(block, shard - block * k))
            if used == 0:
                continue
            rows = slice(block * k, block * k + used)
            part = got_ref[2 * k + c].astype(f32)[:used]
            for j in range(slots):
                dst = slice(step * j + half * c, step * j + half * (c + 1))
                gate_ref[rows, dst] = part[:, half * j : half * (j + 1)]
                up_ref[rows, dst] = part[:, ff // 2 + half * j : ff // 2 + half * (j + 1)]
            if c == 0:
                o_ref[rows, :split] = part[:, packed:]
            else:
                o_ref[rows, split:] = part[:, packed : packed + width - split]
            scr[rows, :] = part[:, ff:packed]
        down = unpack_down(scr[:shard, :], width)
        down_ref[:, half * c : half * (c + 1)] = down.T


def finish_kernel(chips, order_ref, *refs):
    mine, theirs = refs[:chips], refs[chips : 2 * chips]
    qg_ref, kg_ref, vg_ref, gg_ref, parts_scr = refs[2 * chips :]
    core = order_ref[0]
    place = order_ref[1]
    step = mine[0].shape[0]
    for k in range(chips):
        at = pl.multiple_of(lax.rem(place + chips - k, chips) * step, 16)
        parts_scr[core, pl.ds(at, step), :] = mine[k][...]
        parts_scr[1 - core, pl.ds(at, step), :] = theirs[k][...]
    shard, width = qg_ref.shape
    kv_width = kg_ref.shape[0]
    cut = parts_scr.shape[2]
    rest = 2 * kv_width + width - cut
    qg_ref[:, :cut] = parts_scr[0, :shard, :].astype(f32)
    qg_ref[:, cut:] = parts_scr[1, :shard, 2 * kv_width : rest].astype(f32)
    kv = parts_scr[1, :, : 2 * kv_width].astype(f32).T
    kg_ref[...] = kv[:kv_width, :shard]
    vg_ref[...] = kv[kv_width:, :shard]
    gg_ref[...] = parts_scr[1, :, rest:].astype(f32).T[:8, :shard]


def moves(fsdp, ctx, target):
    pairs = []
    for f in range(fsdp):
        for c in range(ctx):
            to_f, to_c = target(f, c)
            if 0 <= to_c < ctx:
                pairs.append((f * ctx + c, to_f * ctx + to_c))
    return pairs


def plus(a, b):
    return (a.astype(f32) + b.astype(f32)).astype(bf16)


def program(
    fsdp, ctx,
    block_input, query_weight, key_matrix, value_matrix, out_weight, gate_weight, up_weight,
    down_weight, attention_gain, feedforward_gain, cotangent,
):
    chips = ctx // 2
    paired = fsdp == 4
    sibling = moves(fsdp, ctx, lambda f, c: (f, c ^ 1))
    up_z = moves(fsdp, ctx, lambda f, c: (f, c + 2))
    down_z = moves(fsdp, ctx, lambda f, c: (f, c - 2))
    near = moves(fsdp, ctx, lambda f, c: (f ^ (1 + c % 2), c))
    far = moves(fsdp, ctx, lambda f, c: (f ^ (2 - c % 2), c))
    rotations = [
        moves(fsdp, ctx, lambda f, c, k=k: (f, (c + 2 * k) % ctx)) for k in range(chips)
    ]
    columns = [[c + 2 * z for z in range(chips)] for c in range(2)]
    rank = lax.axis_index("ctx")
    core, place = rank % 2, rank // 2
    spot = lax.axis_index("fsdp")
    _, half, width = block_input.shape
    rows = 2 * half
    kv_width = KEY_HEAD_COUNT * HEAD_DIM
    shard = width // fsdp
    ff = gate_weight.shape[1]
    parts = fsdp if paired else 1

    def send(value, pairs):
        return lax.ppermute(value, AXES, pairs)

    ids = jnp.arange(fsdp, dtype=jnp.int32)
    if paired:
        first_order = jnp.bitwise_xor(spot, ids)
        second_order = jnp.bitwise_xor(spot, jnp.array([0, 2, 1, 3], jnp.int32))
        second_slot = jnp.where(first_order == 1, 2, jnp.where(first_order == 2, 1, first_order))
        order = [core[None], first_order, second_order, first_order, second_slot]
    else:
        order = [core[None], ids, ids, ids, ids]
    order = jnp.concatenate([o.astype(jnp.int32) for o in order])
    where = jnp.stack([core, place]).astype(jnp.int32)

    def gather(item, axis=0):
        if not paired:
            return [lax.all_gather(item, "fsdp", axis=axis, tiled=True)]
        a = send(item, near)
        b = send(item, far)
        return [item, a, b, send(a, far)]

    x_t = jnp.transpose(block_input, (0, 2, 1))
    cot_t = jnp.transpose(cotangent, (0, 2, 1))

    gains = jnp.pad(jnp.stack([attention_gain, feedforward_gain]), ((0, 14), (0, 0)))
    item, x_send = call(
        first_kernel,
        [((kv_width + 16, shard), bf16), ((width, half), bf16)],
        (where, x_t, key_matrix.T, value_matrix.T, gains),
        0,
        scratch=[pltpu.SemaphoreType.DMA],
        smem=1,
        hbm=(1,),
    )
    x_got = send(x_send, sibling)
    if paired:
        near_got = send(item, near)
        far_got = send(item, far)
        mine = [item, near_got, far_got, send(near_got, far)]
    else:
        mine = gather(item, axis=1)
    theirs = [send(piece, sibling) for piece in mine]
    positions = (place * rows + jnp.arange(rows, dtype=jnp.int32)).astype(f32)
    steps = jnp.arange(HEAD_DIM // 2, dtype=f32)
    angles = (rope_base ** (-2.0 * steps / HEAD_DIM))[:, None] * positions[None, :]
    cos, sin = jnp.cos(angles), jnp.sin(angles)

    xt, n1t, kv, w_kv, gain = call(
        functools.partial(key_kernel, parts, fsdp),
        [
            ((width, rows), bf16),
            ((width, rows), bf16),
            ((rows, 2 * kv_width), bf16),
            ((2, parts, kv_width + 16, width // parts), bf16),
            ((width, 8), f32),
        ],
        (order, x_t, x_got, cos, sin, *mine, *theirs),
        5,
        scratch=[pltpu.SemaphoreType.DMA((2 + 2 * parts,))],
        smem=1,
        hbm=(1, 2, *range(5, 5 + 2 * parts)),
    )
    qo_item, gu_item, down_item = call(
        functools.partial(halves_kernel, fsdp),
        [
            ((shard, width), bf16),
            ((shard, ff), bf16),
            ((down_weight.shape[0] // 2, width), bf16),
        ],
        (where, query_weight, out_weight, gate_weight, up_weight, down_weight.T),
        3,
        smem=1,
        after=(kv,),
    )
    gate_up = lax.all_gather(gu_item, "fsdp", axis=0, tiled=True)

    stat = ((KEY_HEAD_COUNT, 8, rows), f32)
    acc_shape = ((QUERY_HEAD_COUNT, HEAD_DIM, rows), f32)
    key_scratch = pltpu.VMEM((KEY_HEAD_COUNT, rows, HEAD_DIM), bf16)
    turned_scratch = pltpu.VMEM((KEY_HEAD_COUNT, HEAD_DIM, rows), bf16)
    wide_scratch = pltpu.VMEM((KEY_HEAD_COUNT, rows, HEAD_DIM), f32)

    def ok(distance):
        return (place >= distance).astype(jnp.int32)[None]

    def heads(array):
        return leading(array, array.shape[0] // KEY_HEAD_COUNT)

    cot_got = send(cot_t, sibling)
    blocks = [kv]
    blocks.append(send(kv, up_z))
    mine = gather(qo_item)
    theirs = [send(piece, sibling) for piece in mine]
    qt, q, wq, wo = call(
        functools.partial(query_kernel, parts, fsdp),
        [
            ((QUERY_HEAD_COUNT, HEAD_DIM, rows), bf16),
            ((QUERY_HEAD_COUNT, rows, HEAD_DIM), bf16),
            ((width, width), bf16),
            ((width, width), bf16),
        ],
        (order, n1t, cos, sin, *mine, *theirs),
        5,
        scratch=[pltpu.SemaphoreType.DMA((2 * parts,))],
        smem=1,
        hbm=range(4, 4 + 2 * parts),
    )
    down_pieces = gather(down_item)
    states = [heads(Out(*stat)), heads(Out(*stat)), heads(Out(*acc_shape))]
    m, l, acc = call_grid(
        forward_diagonal,
        KEY_HEAD_COUNT,
        states,
        (ok(0), heads(qt), whole(kv)),
        8,
        scratch=[key_scratch, turned_scratch],
    )
    for distance in range(1, chips):
        if distance + 1 < chips:
            blocks.append(send(blocks[distance], up_z))
        m, l, acc = call_grid(
            forward_full,
            KEY_HEAD_COUNT,
            states,
            (ok(distance), heads(qt), whole(blocks[distance]), heads(m), heads(l), heads(acc)),
            10,
            scratch=[key_scratch, turned_scratch],
            after=(cot_got, *down_pieces[1:3]) if distance == chips - 1 else (),
        )

    att, middle, n2 = call(
        middle_kernel,
        [((width, rows), bf16), ((width, rows), f32), ((width, rows), bf16)],
        (xt, acc, l, wo, gain),
        4,
        after=down_pieces[3:],
    )

    n2_got = send(n2, sibling)
    groups = 2 if paired else 1
    per = fsdp // groups
    half_ff = ff // 2
    tile = 256
    ff_out = call(
        functools.partial(ff_kernel, parts, fsdp, groups, tile),
        [((width, rows), f32), ((width, rows), f32), ((2 * width, rows), bf16)]
        + [((per, shard, ff + half_ff), bf16)] * groups,
        (order, gate_up, *down_pieces, n2, n2_got, cot_t, cot_got),
        37,
        scratch=[
            pltpu.VMEM((width, ff), bf16),
            pltpu.VMEM((half_ff, width), bf16),
            pltpu.VMEM((2 * rows, width), bf16),
            pltpu.VMEM((width, 2 * rows), bf16),
            pltpu.VMEM((2 * rows, width), bf16),
            pltpu.VMEM((width, 2 * rows), bf16),
            pltpu.VMEM((2 * rows, width), f32),
            pltpu.VMEM((2 * rows, width), f32),
            pltpu.VMEM((fsdp, shard, ff + half_ff), bf16),
            pltpu.VMEM((half_ff, width), bf16),
            pltpu.SemaphoreType.DMA((7 + parts,)),
            pltpu.SemaphoreType.DMA((groups,)),
        ],
        smem=1,
        hbm=range(1, 6 + parts),
        outs_hbm=range(3, 3 + groups),
        vmem=LARGE,
    )
    ff_sum, gn, ff_send = ff_out[:3]
    ff_terms = ff_out[3:]
    ff_got = send(ff_send, sibling)

    split = 512
    if paired:
        ff_far = send(ff_terms[1], far)

    def one_half(array):
        return trailing(array, half)

    def cot_of(array, mine):
        return (array, (1, width, half), lambda i, s: (s[0], 0, 0))

    fin, grad_middle, o_keep, o_send, do, dot_t, delta, lse, gain_two_term = call_grid(
        functools.partial(turn_kernel, fsdp),
        2,
        [
            one_half(Out((width, rows), bf16)),
            one_half(Out((width, rows), f32)),
            whole(Out((fsdp, shard, split), bf16)),
            whole(Out((fsdp, shard, split), bf16)),
            (
                Out((QUERY_HEAD_COUNT, rows, HEAD_DIM), bf16),
                (QUERY_HEAD_COUNT, half, HEAD_DIM),
                lambda i, s: (0, i, 0),
            ),
            one_half(Out((QUERY_HEAD_COUNT, HEAD_DIM, rows), bf16)),
            one_half(Out(*stat)),
            one_half(Out(*stat)),
            whole(Out((width, 8), f32)),
        ],
        (
            order, one_half(middle), one_half(ff_sum), one_half(gn), one_half(ff_got), whole(gain),
            cot_of(cot_t, True), cot_of(cot_got, False), whole(wo), one_half(att), one_half(acc),
            one_half(m), one_half(l),
        ),
        11,
        scratch=[pltpu.VMEM((width, width), f32), pltpu.VMEM((width, 8), f32)],
    )

    def added(a, b, count, after=()):
        lead = a.shape[0] // count
        shape = a.shape if count == 1 else (a.shape[1:] if lead == 1 else (lead, *a.shape[1:]))
        return call(add_kernel, [(shape, bf16)] * count, (a, b), 2, after=after)

    def scatter_row(terms):
        return lax.psum_scatter(terms[0], "fsdp", scatter_dimension=0, tiled=False)

    block = -(-shard // (16 * chips)) * 16

    def scatter_column(pairs, after=()):
        shape = (chips, block, sum(a.shape[1] for a in pairs[::2]))
        (cut_up,) = call(join_kernel, [(shape, bf16)], pairs, 3, after=after)
        part = lax.psum_scatter(
            cut_up, "ctx", scatter_dimension=0, tiled=False, axis_index_groups=columns
        )
        return cut_up, part

    def pull(distance, dq, after):
        first = dq is None
        args = [
            ok(distance), heads(qt), heads(q), heads(dot_t), heads(do), heads(lse), heads(delta),
            whole(blocks[distance]),
        ]
        return call_grid(
            functools.partial(backward_kernel, distance == 0, first),
            KEY_HEAD_COUNT,
            [heads(Out(*acc_shape)), whole(Out((rows, 2 * kv_width), bf16))],
            args if first else args + [heads(dq)],
            14,
            scratch=[key_scratch, key_scratch, turned_scratch, wide_scratch, wide_scratch],
            after=after,
        )

    o_got = send(o_send, sibling)
    dq, dkv = pull(chips - 1, None, ())
    if not paired:
        halves = [scatter_row(ff_terms), scatter_row(added(o_keep, o_got, 1))]
        pairs = [a for term in halves for a in (term, jnp.zeros_like(term))]
        joined, part = scatter_column(pairs)
    waits = ()
    for distance in reversed(range(1, chips)):
        coming = send(dkv, down_z)
        done = chips - 1 - distance
        if paired and done == 0:
            o_terms = added(o_keep, o_got, 2, (dq,))
            o_far = send(o_terms[1], far)
            waits += (o_terms[1],)
        if paired and done == 1:
            ff_half = added(ff_terms[0], ff_far, 2, (dq,))
            ff_back = send(ff_half[1], near)
            o_half = added(o_terms[0], o_far, 2, (dq,))
            o_back = send(o_half[1], near)
            waits += (ff_half[1], o_half[1])
        if paired and distance == 1:
            joined, part = scatter_column((ff_half[0], ff_back, o_half[0], o_back), (dq, dkv))
            waits += (joined,)
        dq, dkv = pull(distance - 1, dq, waits)
        waits = ()
        if distance > 1:
            (dkv,) = added(dkv, coming, 1)
            waits = (dkv,)

    cut = 896
    rest = 2 * kv_width + width - cut
    input_grad, keep, other = call_grid(
        functools.partial(last_kernel, parts, fsdp),
        2,
        [
            one_half(Out((width, rows), bf16)),
            whole(Out((fsdp, shard, cut), bf16)),
            whole(Out((fsdp, shard, cut), bf16)),
        ],
        (
            order, one_half(dq), leading(dkv, half), leading(coming, half), one_half(n1t), whole(wq),
            whole(w_kv), one_half(cos), one_half(sin), one_half(xt), whole(gain),
            one_half(grad_middle), whole(gain_two_term),
        ),
        9,
        scratch=[
            pltpu.VMEM((width, half), bf16),
            pltpu.VMEM((rest, half), bf16),
            pltpu.VMEM((width, half), f32),
            pltpu.VMEM((width, cut), f32),
            pltpu.VMEM((width, rest), f32),
            pltpu.VMEM((width, 8), f32),
        ],
    )
    (part,) = call(sum_kernel, [(part.shape, bf16)], (part,), 1, after=(keep,))
    ff_total = lax.all_gather(part, "ctx", axis=0, tiled=False)
    other = send(other, sibling)
    if paired:
        terms = added(keep, other, 2)
        a, b = added(terms[0], send(terms[1], far), 2)
        b = send(b, near)
    else:
        a = scatter_row(added(keep, other, 1))
        b = jnp.zeros_like(a)

    pieces = call(
        functools.partial(add_pieces_kernel, chips),
        [((block, cut), bf16)] * chips,
        (where, a, b),
        1,
        scratch=[pltpu.VMEM((block * chips, cut), f32)],
        smem=1,
    )
    got = [send(pieces[k], rotations[k]) for k in range(1, chips)]
    (total,) = call(sum_kernel, [((block, cut), bf16)], (pieces[0], *got), 1)
    pieces = [total] + [send(total, rotations[k]) for k in range(1, chips)]
    other_pieces = [send(piece, sibling) for piece in pieces]
    query_grad, key_grad, value_grad, gain_grads = call(
        functools.partial(finish_kernel, chips),
        [
            ((shard, width), f32),
            ((kv_width, shard), f32),
            ((kv_width, shard), f32),
            ((8, shard), f32),
        ],
        (where, *pieces, *other_pieces),
        1,
        scratch=[pltpu.VMEM((2, block * chips, cut), bf16)],
        smem=1,
    )
    gate_grad, up_grad, down_grad, out_grad = call(
        functools.partial(finish_ff_kernel, fsdp),
        [
            ((shard, ff), f32),
            ((shard, ff), f32),
            ((width, ff // fsdp), f32),
            ((shard, width), f32),
        ],
        (ff_total,),
        1,
        scratch=[pltpu.VMEM((block * chips, half_ff), f32)],
    )

    def scatter_sequence(block):
        keep = lax.dynamic_slice_in_dim(block, core * half, half, 1)
        got = send(lax.dynamic_slice_in_dim(block, (1 - core) * half, half, 1), sibling)
        both = jnp.stack([jnp.where(core == 0, keep, got), jnp.where(core == 0, got, keep)])
        return jnp.transpose(both, (0, 2, 1))

    return (
        scatter_sequence(fin),
        scatter_sequence(input_grad),
        query_grad,
        key_grad.T,
        value_grad.T,
        out_grad,
        gate_grad,
        up_grad,
        down_grad.T,
        gain_grads[0],
        gain_grads[1],
    )


def solution(mesh):
    in_specs = (
        P("fsdp", "ctx", None),
        P("fsdp", None),
        P("fsdp", None),
        P("fsdp", None),
        P("fsdp", None),
        P("fsdp", None),
        P("fsdp", None),
        P("fsdp", None),
        P("fsdp"),
        P("fsdp"),
        P("fsdp", "ctx", None),
    )
    out_specs = (
        P("fsdp", "ctx", None),
        P("fsdp", "ctx", None),
        P("fsdp", None),
        P("fsdp", None),
        P("fsdp", None),
        P("fsdp", None),
        P("fsdp", None),
        P("fsdp", None),
        P("fsdp", None),
        P("fsdp"),
        P("fsdp"),
    )
    body = functools.partial(program, mesh.shape["fsdp"], mesh.shape["ctx"])
    return jax.shard_map(body, mesh=mesh, in_specs=in_specs, out_specs=out_specs, check_vma=False)
```

time: 500 us -> 407 us (0.81)
  waiting for transfers between devices: 215 us -> 166 us
  other arithmetic: 29.9 us -> 4.63 us
  Pallas kernels: 123 us -> 112 us
  local copies, waits for them, and re-layouts: 54.6 us -> 47.2 us
    psum x1 -> x0, waiting for transfers between devices: 74.2 us -> none  [program(): lax.psum((gu_part, down_part, o_part), 'ctx', axis_index_groups=columns)]
    reduce_scatter x0 -> x1, waiting for transfers between devices: none -> 37.2 us  [scatter_column(): lax.psum_scatter(cut_up, 'ctx', scatter_dimension=0, tiled=False, axis_in...]
    convert_element_type x13 -> x0, other arithmetic: 17.9 us -> none  [the longest x12 16.9 us: plus(): return (a.astype(f32) + b.astype(f32)).astype(bf16)]
    unnamed x101 -> x174, local copies, waits for them, and re-layouts: 31.4 us -> 44.4 us
    ppermute x53 -> x47, waiting for transfers between devices: 141 us -> 129 us  [send(): return lax.ppermute(value, AXES, pairs)]
    pallas_call x17 -> x29, Pallas kernels: 123 us -> 112 us  [the longest x19 65.9 us: call(): pl.pallas_call(body, out_shape=shapes, in_specs=specs, out_specs=[pl.Bloc...]
    ppermute x4 -> x0, local copies, waits for them, and re-layouts: 8.74 us -> none  [send(): return lax.ppermute(value, AXES, pairs)]
    ppermute x53 -> x47, starting transfers between devices: 52.8 us -> 56.8 us  [send(): return lax.ppermute(value, AXES, pairs)]
  transfers between devices with their start and end apart: 54 -> 50, of which waited for: 20 -> 23; matrix products, arithmetic and copies ran while one was open for 13% -> 2% of each run, Pallas kernels for 16% -> 14%
where the time goes in v2:
time: 407 us; the launch traced here: 402 us
  waiting for transfers between devices  166 us (41%)
  Pallas kernels  112 us (28%)
  starting transfers between devices  57 us (14%)
  local copies, waits for them, and re-layouts  47.2 us (12%)
  between operations  15.1 us (4%)
  other arithmetic  4.63 us (1%)
    ppermute x47, waiting for transfers between devices, send(): return lax.ppermute(value, AXES, pairs)  129 us
    pallas_call x19, Pallas kernels, call(): pl.pallas_call(body, out_shape=shapes, in_specs=specs, out_specs=[pl.Bloc...  65.9 us
    ppermute x47, starting transfers between devices, send(): return lax.ppermute(value, AXES, pairs)  56.8 us
    pallas_call x10, Pallas kernels, call_grid(): pl.pallas_call(body, out_shape=[jax.ShapeDtypeStruct(shape, kind) for (sh...  45.8 us
    unnamed x174, local copies, waits for them, and re-layouts  44.4 us
    reduce_scatter x1, waiting for transfers between devices, scatter_column(): lax.psum_scatter(cut_up, 'ctx', scatter_dimension=0, tiled=False, axis_in...  37.2 us
  transfers between devices with their start and end apart: 50, of which 23 were waited for; matrix products, arithmetic and copies ran while one was open for 2% of the time, Pallas kernels for 14%

profile of v2, /device:TPU:0, one launch (start us, length us, event | category | flops | bytes accessed | tf_op | source)
XLA Modules:
  0.0 401.9 jit_solution(13661107759024794178)
XLA Ops:
  28.3 4.2 %shard_map.204 = (bf16[960,512]{1,0:T(8,128)(2,1)S(1)}, bf16[960,512]{1,0:T(8,128)(2,1)S(1)}, bf16[512,640]{1,0:T(8,128)(2,1)S(1)}, bf16[2,4,336,240]{3,2,1,0:T(8,128)(2,1)S(1)}, f32[960,8]{1,0:T(8,128)S(1)}) custom-call(s32[17]{0:T(128)S(1)} %concatenate.3.refs_0_, bf16[2,960,256]{2,1,0:T(8,128)(2,1)S(1)} %bitcast.32, ...), custom_call_target="tpu_custom_call" | custom-call | flops 5750000128 | tf_op jit(solution)/shard_map/pallas_call | solution.py:50
  39.7 4.4 %collective-permute-start.15 = (bf16[512,640]{1,0:T(8,128)(2,1)S(1)}, bf16[512,640]{1,0:T(8,128)(2,1)}, u32[]{:S(2)}, u32[]{:S(2)}) collective-permute-start(bf16[512,640]{1,0:T(8,128)(2,1)S(1)} %get-tuple-element.91.refs_6_.refs_2_.refs_7_), channel_id=1, source_target_pairs={{0,2},{1,3},{2,4},{3,5},{4,6},{5,7},{8,10},{9,11},{10,12},{11,13},... | collective-permute-start | bytes 1966088 | tf_op jit(solution)/shard_map/ppermute | solution.py:764
  48.3 8.3 %collective-permute-done.15.refs_2_.refs_7_ = bf16[512,640]{1,0:T(8,128)(2,1)} collective-permute-done((bf16[512,640]{1,0:T(8,128)(2,1)S(1)}, bf16[512,640]{1,0:T(8,128)(2,1)}, u32[]{:S(2)}, u32[]{:S(2)}) %collective-permute-start.15) | collective-permute-done | bytes 655392 | tf_op jit(solution)/shard_map/ppermute | solution.py:764
  56.6 5.3 %collective-permute-start.16 = (bf16[512,640]{1,0:T(8,128)(2,1)}, bf16[512,640]{1,0:T(8,128)(2,1)}, u32[]{:S(2)}, u32[]{:S(2)}) collective-permute-start(bf16[512,640]{1,0:T(8,128)(2,1)} %collective-permute-done.15.refs_2_.refs_7_), channel_id=1, source_target_pairs={{0,2},{1,3},{2,4},{3,5},{4,6},{5,7},{8,10},{9,11},{10,12},{11,13},... | collective-permute-start | bytes 1966088 | tf_op jit(solution)/shard_map/ppermute | solution.py:764
  64.7 10.3 %collective-permute-done.10.refs_7_ = bf16[240,960]{1,0:T(8,128)(2,1)} collective-permute-done((bf16[240,960]{1,0:T(8,128)(2,1)}, bf16[240,960]{1,0:T(8,128)(2,1)}, u32[]{:S(2)}, u32[]{:S(2)}) %collective-permute-start.10) | collective-permute-done | bytes 460832 | tf_op jit(solution)/shard_map/ppermute | solution.py:764
  85.8 4.9 %shard_map.206 = (bf16[15,64,512]{2,1,0:T(8,128)(2,1)S(1)}, bf16[15,512,64]{2,1,0:T(8,128)(2,1)S(1)}, bf16[960,960]{1,0:T(8,128)(2,1)S(1)}, bf16[960,960]{1,0:T(8,128)(2,1)S(1)}) custom-call(s32[17]{0:T(128)S(1)} %concatenate.3.refs_0_, bf16[960,512]{1,0:T(8,128)(2,1)S(1)} %copy-done.66, f32[32,512]{1,0:T(8,128)S(1)} %get-tuple-element.170.refs_3_.refs_2_.refs_7_, ...), custom_call_target="tpu_custom_call" | custom-call | flops 5750000128 | tf_op jit(solution)/shard_map/pallas_call | solution.py:50
  93.3 9.3 %shard_map.207 = (f32[5,8,512]{2,1,0:T(8,128)S(1)}, f32[5,8,512]{2,1,0:T(8,128)S(1)}, f32[15,64,512]{2,1,0:T(8,128)S(1)}) custom-call(s32[1]{0:T(128)} %bitcast.9.refs_0_, bf16[15,64,512]{2,1,0:T(8,128)(2,1)S(1)} %get-tuple-element.93.refs_1_, bf16[512,640]{1,0:T(8,128)(2,1)S(1)} %get-tuple-element.91.refs_6_.refs_2_.refs_7_), custom_call_target="tpu_custom_call" | custom-call | flops 9200000000 | tf_op jit(solution)/shard_map/pallas_call | solution.py:73
  106.7 14.1 %collective-permute-done.21.refs_5_ = bf16[320,960]{1,0:T(8,128)(2,1)S(1)} collective-permute-done((bf16[320,960]{1,0:T(8,128)(2,1)S(1)}, bf16[320,960]{1,0:T(8,128)(2,1)S(1)}, u32[]{:S(2)}, u32[]{:S(2)}) %collective-permute-start.21) | collective-permute-done | bytes 614432 | tf_op jit(solution)/shard_map/ppermute | solution.py:764
  127.7 39.0 %shard_map.212 = (f32[960,512]{1,0:T(8,128)}, f32[960,512]{1,0:T(8,128)}, bf16[1920,512]{1,0:T(8,128)(2,1)}, bf16[2,240,3840]{2,1,0:T(8,128)(2,1)}, bf16[2,240,3840]{2,1,0:T(8,128)(2,1)}) custom-call(s32[17]{0:T(128)} %copy-done.12, bf16[960,2560]{1,0:T(8,128)(2,1)} %all-gather.4.cloned.1.call-done.refs_1_, bf16[320,960]{1,0:T(8,128)(2,1)} %copy-done.25, ...), custom_call_target="tpu_custom_call" | custom-call | flops 42550001664 | tf_op jit(solution)/shard_map/pallas_call | solution.py:50
  179.2 10.3 %shard_map.213 = (bf16[960,512]{1,0:T(8,128)(2,1)S(1)}, f32[960,512]{1,0:T(8,128)S(1)}, bf16[4,240,512]{2,1,0:T(8,128)(2,1)S(1)}, bf16[4,240,512]{2,1,0:T(8,128)...) custom-call(s32[17]{0:T(128)S(1)} %copy-done.13, ...), custom_call_target="tpu_custom_call" | custom-call | flops 12650000384 | tf_op jit(solution)/shard_map/pallas_call | solution.py:73
  196.9 14.6 %collective-permute-done.26.refs_1_ = bf16[512,640]{1,0:T(8,128)(2,1)S(1)} collective-permute-done((bf16[512,640]{1,0:T(8,128)(2,1)S(1)}, bf16[512,640]{1,0:T(8,128)(2,1)S(1)}, u32[]{:S(2)}, u32[]{:S(2)}) %collective-permute-start.26) | collective-permute-done | bytes 655392 | tf_op jit(solution)/shard_map/ppermute | solution.py:764
  218.7 14.5 %collective-permute-done.29.refs_1_ = bf16[512,640]{1,0:T(8,128)(2,1)S(1)} collective-permute-done((bf16[512,640]{1,0:T(8,128)(2,1)S(1)}, bf16[512,640]{1,0:T(8,128)(2,1)S(1)}, u32[]{:S(2)}, u32[]{:S(2)}) %collective-permute-start.29) | collective-permute-done | bytes 655392 | tf_op jit(solution)/shard_map/ppermute | solution.py:764
  233.4 7.0 %collective-permute-done.31.refs_3_ = bf16[240,512]{1,0:T(8,128)(2,1)S(1)} collective-permute-done((bf16[240,512]{1,0:T(8,128)(2,1)S(1)}, bf16[240,512]{1,0:T(8,128)(2,1)S(1)}, u32[]{:S(2)}, u32[]{:S(2)}) %collective-permute-start.31) | collective-permute-done | bytes 245792 | tf_op jit(solution)/shard_map/ppermute | solution.py:764
  250.9 10.8 %shard_map.223 = (f32[15,64,512]{2,1,0:T(8,128)S(1)}, bf16[512,640]{1,0:T(8,128)(2,1)S(1)}) custom-call(s32[1]{0:T(128)} %bitcast.9.refs_0_, bf16[15,64,512]{2,1,0:T(8,128)(2,1)S(1)} %copy-done.70, bf16[15,512,64]{2,1,0:T(8,128)(2,1)S(1)} %copy-done.59, bf16[15,64,512]{2,1,0:T(8,128)(2,1)S(1)} %copy-done.78, bf16[15,512,64]{2,1,0:T(8,128)(2,1)S(1)} %copy-done.74, ...), custom_call_target="tpu_custom_call" | custom-call | flops 16099999744 | tf_op jit(solution)/shard_map/pallas_call | solution.py:73
  261.7 6.1 %collective-permute-done.32.refs_3_ = bf16[512,640]{1,0:T(8,128)(2,1)S(1)} collective-permute-done((bf16[512,640]{1,0:T(8,128)(2,1)S(1)}, bf16[512,640]{1,0:T(8,128)(2,1)S(1)}, u32[]{:S(2)}, u32[]{:S(2)}) %collective-permute-start.32) | collective-permute-done | bytes 655392 | tf_op jit(solution)/shard_map/ppermute | solution.py:764
  267.8 8.4 %shard_map.224 = (bf16[960,512]{1,0:T(8,128)(2,1)S(1)}, bf16[4,240,896]{2,1,0:T(8,128)(2,1)S(1)}, bf16[4,240,896]{2,1,0:T(8,128)(2,1)S(1)}) custom-call(s32[17]{0:T(128)S(1)} %copy-done.13, f32[15,64,512]{2,1,0:T(8,128)S(1)} %get-tuple-element.138.refs_1_, bf16[512,640]{1,0:T(8,128)(2,1)S(1)} %get-tuple-element.139.refs_2_, ...), custom_call_target="tpu_custom_call" | custom-call | flops 10350000128 | tf_op jit(solution)/shard_map/pallas_call | solution.py:73
  278.6 37.2 %reduce-scatter.2.cloned.1.call-done = bf16[1,64,4352]{2,1,0:T(8,128)(2,1)} async-done(((bf16[4,64,4352]{2,1,0:T(8,128)(2,1)}), bf16[1,64,4352]{2,1,0:T(8,128)(2,1)}) %reduce-scatter.2.cloned.1.call-update) | async-done | bytes 557072 | tf_op jit(solution)/shard_map/reduce_scatter | solution.py:985
  319.4 3.7 collective-permute-done.34.refs_1_
  328.7 10.8 %collective-permute-done.35.refs_1_ = bf16[2,240,896]{2,1,0:T(8,128)(2,1)S(1)} collective-permute-done((bf16[2,240,896]{2,1,0:T(8,128)(2,1)}, bf16[2,240,896]{2,1,0:T(8,128)(2,1)S(1)}, u32[]{:S(2)}, u32[]{:S(2)}) %collective-permute-start.35) | collective-permute-done | bytes 860192 | tf_op jit(solution)/shard_map/ppermute | solution.py:764
  344.6 5.3 %collective-permute-done.36.refs_2_ = bf16[240,896]{1,0:T(8,128)(2,1)S(1)} collective-permute-done((bf16[240,896]{1,0:T(8,128)(2,1)S(1)}, bf16[240,896]{1,0:T(8,128)(2,1)S(1)}, u32[]{:S(2)}, u32[]{:S(2)}) %collective-permute-start.36) | collective-permute-done | bytes 430112 | tf_op jit(solution)/shard_map/ppermute | solution.py:764
  356.7 4.3 %collective-permute-done.37.refs_1_ = bf16[64,896]{1,0:T(8,128)(2,1)S(1)} collective-permute-done((bf16[64,896]{1,0:T(8,128)(2,1)S(1)}, bf16[64,896]{1,0:T(8,128)(2,1)S(1)}, u32[]{:S(2)}, u32[]{:S(2)}) %collective-permute-start.37) | collective-permute-done | bytes 114720 | tf_op jit(solution)/shard_map/ppermute | solution.py:764
  360.9 6.9 %collective-permute-done.38.refs_2_ = bf16[64,896]{1,0:T(8,128)(2,1)S(1)} collective-permute-done((bf16[64,896]{1,0:T(8,128)(2,1)S(1)}, bf16[64,896]{1,0:T(8,128)(2,1)S(1)}, u32[]{:S(2)}, u32[]{:S(2)}) %collective-permute-start.38) | collective-permute-done | bytes 114720 | tf_op jit(solution)/shard_map/ppermute | solution.py:764
  367.9 7.6 %collective-permute-start.40 = (bf16[64,896]{1,0:T(8,128)(2,1)S(1)}, bf16[64,896]{1,0:T(8,128)(2,1)S(1)}, u32[]{:S(2)}, u32[]{:S(2)}) collective-permute-start(bf16[64,896]{1,0:T(8,128)(2,1)S(1)} %shard_map.228.refs_1_), channel_id=1, source_target_pairs={{0,2},{1,3},{2,4},{3,5},{4,6},{5,7},{6,0},{7,1},{8,10},{9,11},{10,... | collective-permute-start | bytes 344072 | tf_op jit(solution)/shard_map/ppermute | solution.py:764
  390.4 4.5 %shard_map.231 = (f32[240,2560]{1,0:T(8,128)}, f32[240,2560]{1,0:T(8,128)}, f32[960,640]{1,0:T(8,128)}, f32[240,960]{1,0:T(8,128)}) custom-call(bf16[8,64,4352]{2,1,0:T(8,128)(2,1)S(1)} %bitcast.30), custom_call_target="tpu_custom_call" | custom-call | flops 1150000000 | tf_op jit(solution)/shard_map/pallas_call | solution.py:50
  (299 shorter events, 134.8 us)
Async XLA Ops:
  7.2 120.5 %all-gather.4.cloned.1.call-start = ((), (), s32[]{:S(2)}) async-start(), calls=%async_computation.1 | async-start | bytes 6144000 | tf_op jit(solution)/shard_map/all_gather | solution.py:837
  39.6 276.2 %reduce-scatter.2.cloned.1.call-start = ((), (), s32[]{:S(2)}) async-start(), calls=%async_computation.2 | async-start | bytes 2785280 | tf_op jit(solution)/shard_map/reduce_scatter | solution.py:985
  39.7 16.9 %collective-permute-start.15 = (bf16[512,640]{1,0:T(8,128)(2,1)S(1)}, bf16[512,640]{1,0:T(8,128)(2,1)}, u32[]{:S(2)}, u32[]{:S(2)}) collective-permute-start(bf16[512,640]{1,0:T(8,128)(2,1)S(1)} %get-tuple-element.91.refs_6_.refs_2_.refs_7_), channel_id=1, source_target_pairs={{0,2},{1,3},{2,4},{3,5},{4,6},{5,7},{8,10},{9,11},{10,12},{11,13},... | collective-permute-start | bytes 1966088 | tf_op jit(solution)/shard_map/ppermute | solution.py:764
  44.0 19.4 %collective-permute-start.9 = (bf16[240,960]{1,0:T(8,128)(2,1)}, bf16[240,960]{1,0:T(8,128)(2,1)}, u32[]{:S(2)}, u32[]{:S(2)}) collective-permute-start(bf16[240,960]{1,0:T(8,128)(2,1)} %get-tuple-element.92.refs_4_), channel_id=1, source_target_pairs={{0,16},{1,9},{2,18},{3,11},{4,20},{5,13},{6,22},{7,15},{8,24},{9,1... | collective-permute-start | bytes 1382408 | tf_op jit(solution)/shard_map/ppermute | solution.py:764
  44.8 18.7 %collective-permute-start.11 = (bf16[240,960]{1,0:T(8,128)(2,1)}, bf16[240,960]{1,0:T(8,128)(2,1)S(1)}, u32[]{:S(2)}, u32[]{:S(2)}) collective-permute-start(bf16[240,960]{1,0:T(8,128)(2,1)} %get-tuple-element.92.refs_4_), channel_id=1, source_target_pairs={{0,1},{1,0},{2,3},{3,2},{4,5},{5,4},{6,7},{7,6},{8,9},{9,8},{10,11... | collective-permute-start | bytes 1382408 | tf_op jit(solution)/shard_map/ppermute | solution.py:764
  47.5 27.5 %collective-permute-start.10 = (bf16[240,960]{1,0:T(8,128)(2,1)}, bf16[240,960]{1,0:T(8,128)(2,1)}, u32[]{:S(2)}, u32[]{:S(2)}) collective-permute-start(bf16[240,960]{1,0:T(8,128)(2,1)} %collective-permute-done.8.refs_5_), channel_id=1, source_target_pairs={{0,16},{1,9},{2,18},{3,11},{4,20},{5,13},{6,22},{7,15},{8,24},{9,1... | collective-permute-start | bytes 1382408 | tf_op jit(solution)/shard_map/ppermute | solution.py:764
  56.6 23.8 %collective-permute-start.16 = (bf16[512,640]{1,0:T(8,128)(2,1)}, bf16[512,640]{1,0:T(8,128)(2,1)}, u32[]{:S(2)}, u32[]{:S(2)}) collective-permute-start(bf16[512,640]{1,0:T(8,128)(2,1)} %collective-permute-done.15.refs_2_.refs_7_), channel_id=1, source_target_pairs={{0,2},{1,3},{2,4},{3,5},{4,6},{5,7},{8,10},{9,11},{10,12},{11,13},... | collective-permute-start | bytes 1966088 | tf_op jit(solution)/shard_map/ppermute | solution.py:764
  61.9 15.4 %collective-permute-start.19 = (bf16[320,960]{1,0:T(8,128)(2,1)S(1)}, bf16[320,960]{1,0:T(8,128)(2,1)S(1)}, u32[]{:S(2)}, u32[]{:S(2)}) collective-permute-start(bf16[320,960]{1,0:T(8,128)(2,1)S(1)} %get-tuple-element.103.refs_2_), channel_id=1, source_target_pairs={{0,8},{1,17},{2,10},{3,19},{4,12},{5,21},{6,14},{7,23},{8,0},{9,25... | collective-permute-start | bytes 1843208 | tf_op jit(solution)/shard_map/ppermute | solution.py:764
  77.3 28.0 %collective-permute-start.18 = (bf16[2,960,256]{2,1,0:T(8,128)(2,1)S(1)}, bf16[2,960,256]{2,1,0:T(8,128)(2,1)S(1)}, u32[]{:S(2)}, u32[]{:S(2)}) collective-permute-start(bf16[2,960,256]{2,1,0:T(8,128)(2,1)S(1)} %bitcast.37), channel_id=1, source_target_pairs={{0,1},{1,0},{2,3},{3,2},{4,5},{5,4},{6,7},{7,6},{8,9},{9,8},{10,11... | collective-permute-start | bytes 2949128 | tf_op jit(solution)/shard_map/ppermute | solution.py:764
  78.4 27.0 %collective-permute-start.20 = (bf16[320,960]{1,0:T(8,128)(2,1)S(1)}, bf16[320,960]{1,0:T(8,128)(2,1)S(1)}, u32[]{:S(2)}, u32[]{:S(2)}) collective-permute-start(bf16[320,960]{1,0:T(8,128)(2,1)S(1)} %get-tuple-element.103.refs_2_), channel_id=1, source_target_pairs={{0,16},{1,9},{2,18},{3,11},{4,20},{5,13},{6,22},{7,15},{8,24},{9,1... | collective-permute-start | bytes 1843208 | tf_op jit(solution)/shard_map/ppermute | solution.py:764
  79.1 41.8 %collective-permute-start.21 = (bf16[320,960]{1,0:T(8,128)(2,1)S(1)}, bf16[320,960]{1,0:T(8,128)(2,1)S(1)}, u32[]{:S(2)}, u32[]{:S(2)}) collective-permute-start(bf16[320,960]{1,0:T(8,128)(2,1)S(1)} %collective-permute-done.19.refs_7_.refs_3_), channel_id=1, source_target_pairs={{0,16},{1,9},{2,18},{3,11},{4,20},{5,13},{6,22},{7,15},{8,24},{9,1... | collective-permute-start | bytes 1843208 | tf_op jit(solution)/shard_map/ppermute | solution.py:764
  80.4 25.0 %collective-permute-start.17 = (bf16[512,640]{1,0:T(8,128)(2,1)}, bf16[512,640]{1,0:T(8,128)(2,1)S(1)}, u32[]{:S(2)}, u32[]{:S(2)}) collective-permute-start(bf16[512,640]{1,0:T(8,128)(2,1)} %collective-permute-done.16.refs_2_.refs_7_), channel_id=1, source_target_pairs={{0,2},{1,3},{2,4},{3,5},{4,6},{5,7},{8,10},{9,11},{10,12},{11,13},... | collective-permute-start | bytes 1966088 | tf_op jit(solution)/shard_map/ppermute | solution.py:764
  166.9 46.4 %collective-permute-start.27 = (bf16[2,240,3840]{2,1,0:T(8,128)(2,1)}, bf16[2,240,3840]{2,1,0:T(8,128)(2,1)S(1)}, u32[]{:S(2)}, u32[]{:S(2)}) collective-permute-start(bf16[2,240,3840]{2,1,0:T(8,128)(2,1)} %get-tuple-element.130), channel_id=1, source_target_pairs={{0,16},{1,9},{2,18},{3,11},{4,20},{5,13},{6,22},{7,15},{8,24},{9,1... | collective-permute-start | bytes 11059208 | tf_op jit(solution)/shard_map/ppermute | solution.py:764
  192.6 18.9 %collective-permute-start.26 = (bf16[512,640]{1,0:T(8,128)(2,1)S(1)}, bf16[512,640]{1,0:T(8,128)(2,1)S(1)}, u32[]{:S(2)}, u32[]{:S(2)}) collective-permute-start(bf16[512,640]{1,0:T(8,128)(2,1)S(1)} %get-tuple-element.128), channel_id=1, source_target_pairs={{2,0},{3,1},{4,2},{5,3},{6,4},{7,5},{10,8},{11,9},{12,10},{13,11},... | collective-permute-start | bytes 1966088 | tf_op jit(solution)/shard_map/ppermute | solution.py:764
  194.5 21.4 %collective-permute-start.28 = (bf16[2,240,512]{2,1,0:T(8,128)(2,1)S(1)}, bf16[2,240,512]{2,1,0:T(8,128)(2,1)S(1)}, u32[]{:S(2)}, u32[]{:S(2)}) collective-permute-start(bf16[2,240,512]{2,1,0:T(8,128)(2,1)S(1)} %get-tuple-element.125.refs_9_), channel_id=1, source_target_pairs={{0,16},{1,9},{2,18},{3,11},{4,20},{5,13},{6,22},{7,15},{8,24},{9,1... | collective-permute-start | bytes 1474568 | tf_op jit(solution)/shard_map/ppermute | solution.py:764
  211.7 21.6 %collective-permute-start.29 = (bf16[512,640]{1,0:T(8,128)(2,1)S(1)}, bf16[512,640]{1,0:T(8,128)(2,1)S(1)}, u32[]{:S(2)}, u32[]{:S(2)}) collective-permute-start(bf16[512,640]{1,0:T(8,128)(2,1)S(1)} %shard_map.217.refs_9_), channel_id=1, source_target_pairs={{2,0},{3,1},{4,2},{5,3},{6,4},{7,5},{10,8},{11,9},{12,10},{13,11},... | collective-permute-start | bytes 1966088 | tf_op jit(solution)/shard_map/ppermute | solution.py:764
  214.4 26.0 %collective-permute-start.30 = (bf16[240,3840]{1,0:T(8,128)(2,1)S(1)}, bf16[240,3840]{1,0:T(8,128)(2,1)S(1)}, u32[]{:S(2)}, u32[]{:S(2)}) collective-permute-start(bf16[240,3840]{1,0:T(8,128)(2,1)S(1)} %get-tuple-element.131.refs_10_), channel_id=1, source_target_pairs={{0,8},{1,17},{2,10},{3,19},{4,12},{5,21},{6,14},{7,23},{8,0},{9,25... | collective-permute-start | bytes 5529608 | tf_op jit(solution)/shard_map/ppermute | solution.py:764
  216.0 24.4 %collective-permute-start.31 = (bf16[240,512]{1,0:T(8,128)(2,1)S(1)}, bf16[240,512]{1,0:T(8,128)(2,1)S(1)}, u32[]{:S(2)}, u32[]{:S(2)}) collective-permute-start(bf16[240,512]{1,0:T(8,128)(2,1)S(1)} %get-tuple-element.133.refs_11_), channel_id=1, source_target_pairs={{0,8},{1,17},{2,10},{3,19},{4,12},{5,21},{6,14},{7,23},{8,0},{9,25... | collective-permute-start | bytes 737288 | tf_op jit(solution)/shard_map/ppermute | solution.py:764
  242.3 145.8 %all-gather.6.cloned.1.call-start = ((), (), s32[]{:S(2)}) async-start(), calls=%async_computation.3 | async-start | bytes 5013504 | tf_op jit(solution)/shard_map/all_gather | solution.py:1061
  242.3 25.4 %collective-permute-start.32 = (bf16[512,640]{1,0:T(8,128)(2,1)S(1)}, bf16[512,640]{1,0:T(8,128)(2,1)S(1)}, u32[]{:S(2)}, u32[]{:S(2)}) collective-permute-start(bf16[512,640]{1,0:T(8,128)(2,1)S(1)} %shard_map.221.refs_5_.refs_9_), channel_id=1, source_target_pairs={{2,0},{3,1},{4,2},{5,3},{6,4},{7,5},{10,8},{11,9},{12,10},{13,11},... | collective-permute-start | bytes 1966088 | tf_op jit(solution)/shard_map/ppermute | solution.py:764
  328.1 15.2 %collective-permute-start.24 = (bf16[960,256]{1,0:T(8,128)(2,1)}, bf16[960,256]{1,0:T(8,128)(2,1)}, u32[]{:S(2)}, u32[]{:S(2)}) collective-permute-start(bf16[960,256]{1,0:T(8,128)(2,1)} %constant_dynamic-slice_fusion.1), channel_id=1, source_target_pairs={{0,1},{1,0},{2,3},{3,2},{4,5},{5,4},{6,7},{7,6},{8,9},{9,8},{10,11... | collective-permute-start | bytes 1474568 | tf_op jit(solution)/shard_map/ppermute | solution.py:764
  343.3 34.7 %collective-permute-start.33 = (bf16[960,256]{1,0:T(8,128)(2,1)S(1)}, bf16[960,256]{1,0:T(8,128)(2,1)S(1)}, u32[]{:S(2)}, u32[]{:S(2)}) collective-permute-start(bf16[960,256]{1,0:T(8,128)(2,1)S(1)} %constant_dynamic-slice_fusion), channel_id=1, source_target_pairs={{0,1},{1,0},{2,3},{3,2},{4,5},{5,4},{6,7},{7,6},{8,9},{9,8},{10,11... | collective-permute-start | bytes 1474568 | tf_op jit(solution)/shard_map/ppermute | solution.py:764
  350.7 17.2 %collective-permute-start.38 = (bf16[64,896]{1,0:T(8,128)(2,1)S(1)}, bf16[64,896]{1,0:T(8,128)(2,1)S(1)}, u32[]{:S(2)}, u32[]{:S(2)}) collective-permute-start(bf16[64,896]{1,0:T(8,128)(2,1)S(1)} %get-tuple-element.153), channel_id=1, source_target_pairs={{0,4},{1,5},{2,6},{3,7},{4,0},{5,1},{6,2},{7,3},{8,12},{9,13},{10,... | collective-permute-start | bytes 344072 | tf_op jit(solution)/shard_map/ppermute | solution.py:764
  352.8 15.1 %collective-permute-start.39 = (bf16[64,896]{1,0:T(8,128)(2,1)S(1)}, bf16[64,896]{1,0:T(8,128)(2,1)S(1)}, u32[]{:S(2)}, u32[]{:S(2)}) collective-permute-start(bf16[64,896]{1,0:T(8,128)(2,1)S(1)} %get-tuple-element.154), channel_id=1, source_target_pairs={{0,6},{1,7},{2,0},{3,1},{4,2},{5,3},{6,4},{7,5},{8,14},{9,15},{10,... | collective-permute-start | bytes 344072 | tf_op jit(solution)/shard_map/ppermute | solution.py:764
  (113 other events, 1282.0 us)
Sparse Core Ops, SparseCore 0:
  39.7 80.5 all-gather.3
  242.4 73.3 reduce-scatter.1
  319.3 58.1 all-gather.5
